TPU v7x, 128 devices: a whole 4x4x4 slice. The times are simulated.
128 devices in a mesh: img: 8 (over z_lo, x), freq: 16 (over z_hi, y, core).
Axes of the slice: x: 4, y: 4, z: 4 (z_hi: 2, z_lo: 2; z = z_hi * 2 + z_lo), core: 2. Of those that a mesh axis runs over, the one named last changes fastest.
Arguments:
- images: bfloat16 [2, 12288, 32768], P(None, 'img', 'freq'), may hold values from -6 to 6
- references: bfloat16 [2, 896, 32768], P(None, 'img', 'freq'), may hold values from -6 to 6
- noise_weight: float32 [32768], P('freq'), may hold values from 0.005 to 0.05
- prior_orient: int32 [12288], P('img'), may hold values from 0 to 895
- segment_brick: int32 [16, 896, 16, 1], P('freq', 'img'), may hold values from 0 to 127; in each aligned block of 1792 rows (0 to 1791, 1792 to 3583, ..., all dimensions but the last counted through in order) at most 35 rows name the same one
- segment_row: int32 [16, 896, 16], P('freq', 'img'), may hold values from 0 to 1999
- segment_kernel: int32 [16, 896, 16], P('freq', 'img'), may hold values from 0 to 7
- kernel_taps: float32 [8, 4], replicated, may hold values from 0.1 to 1
Outputs:
- posterior: float32 [896, 12288], P('freq', 'img')
- volume: float32 [128, 2, 2000, 128], P(('img', 'freq'))
Inputs may be any that keep to these rules, and one draw needn't show every extreme that they name: `segment_brick`: counted in aligned blocks of 1792 segments in the map's order, no brick is named more than 35 times within one block, a bound that some block reaches.
All inputs are finite; a program needn't handle non-finite values.
Results may differ from a plain program's by a relative error of at most 0.014.
Values may be sent and summed in bfloat16 or wider, within the bound.
A program may use at most 128 MiB of HBM per device.

v0:
```python
import jax
import jax.numpy as jnp
from jax import lax
from jax.sharding import PartitionSpec as P

BROWS = 2000


tempering = 0.5
masked_logit = -1e30
contract_last = (((1,), (1,)), ((), ()))


def rows_for(lines, devices):
    spare = -lines.shape[0] % devices
    if not spare:
        return lines
    return jnp.concatenate([lines, jnp.zeros((spare, *lines.shape[1:]), lines.dtype)])


def sum_by_parts(shard, axis):
    lines = shard.reshape(-1, *shard.shape[1:][-1:])
    padded = rows_for(lines, lax.axis_size(axis))
    own = lax.psum_scatter(padded, axis, scatter_dimension=0, tiled=True)
    whole = lax.all_gather(own, axis, axis=0, tiled=True)
    return whole[: len(lines)].reshape(shard.shape)


def spread_taps(values, kernels, kernel_taps):
    phases = kernel_taps.shape[0]
    tap_count = kernel_taps.shape[1]
    member = (kernels[:, None] == jnp.arange(phases, dtype=jnp.int32)[None, :]).astype(
        kernel_taps.dtype
    )
    factors = jnp.dot(member, kernel_taps, precision=lax.Precision.HIGHEST)
    padded = jnp.pad(values, ((0, 0), (0, 0), (tap_count - 2, 1)))
    lane_count = values.shape[2]
    result = jnp.zeros(values.shape, values.dtype)
    for tap_index in range(tap_count):
        first_lane = tap_count - 1 - tap_index
        result = (
            result
            + factors[:, tap_index, None, None] * padded[:, :, first_lane : first_lane + lane_count]
        )
    return result


def window_logits(scores, orient_index, prior_orient, orient_count):
    distance = (orient_index[:, None] - prior_orient[None, :]) % orient_count
    half_window = orient_count // 8
    allowed = (distance <= half_window) | (distance >= orient_count - half_window)
    return jnp.where(allowed, tempering * scores, masked_logit)


def on_device(
    images,
    references,
    noise_weight,
    prior_orient,
    segment_brick,
    segment_row,
    segment_kernel,
    kernel_taps,
):
    image_groups = lax.axis_size("img")
    freq_groups = lax.axis_size("freq")
    local_orients = references.shape[1]
    orient_count = local_orients * image_groups
    share_rows = orient_count // freq_groups
    unpacked = lax.all_gather(references, "img", axis=1, tiled=True).astype(jnp.float32)
    weighted = (noise_weight * unpacked).astype(jnp.bfloat16)
    energies = jnp.sum(
        noise_weight * (unpacked[0] * unpacked[0] + unpacked[1] * unpacked[1]), axis=1
    )
    products = lax.dot_general(
        weighted[0], images[0], contract_last, preferred_element_type=jnp.float32
    )
    products = products + lax.dot_general(
        weighted[1], images[1], contract_last, preferred_element_type=jnp.float32
    )
    partial_scores = products - 0.5 * energies[:, None]
    scores = sum_by_parts(partial_scores, "freq")
    logits = window_logits(
        scores, jnp.arange(orient_count, dtype=jnp.int32), prior_orient, orient_count
    )
    highest = jnp.max(logits, axis=0)
    raised = jnp.exp(logits - highest[None, :])
    posterior = raised / jnp.sum(raised, axis=0)[None, :]
    rounded = posterior.astype(jnp.bfloat16)
    own_rows = lax.dynamic_slice_in_dim(
        posterior, lax.axis_index("freq") * share_rows, share_rows, 0
    )
    weighted_sums = lax.psum_scatter(
        jnp.einsum("oi,cif->ocf", rounded, images, preferred_element_type=jnp.float32).astype(
            jnp.bfloat16
        ),
        "img",
        scatter_dimension=0,
        tiled=True,
    ).astype(jnp.float32)
    segment_blocks = segment_row.shape[2]
    lane_count = images.shape[2] // segment_blocks
    local_segments = local_orients * segment_blocks
    values = weighted_sums.reshape(local_orients, 2, segment_blocks, lane_count).transpose(
        0, 2, 1, 3
    )
    values = values.reshape(local_segments, 2, lane_count)
    targets = segment_brick.reshape(local_segments)
    voxel_rows = segment_row.reshape(local_segments)
    kernels = segment_kernel.reshape(local_segments)
    brick_count = image_groups * freq_groups
    capacity = max(2, 5 * local_segments // (2 * brick_count))
    segment_ids = jnp.arange(local_segments, dtype=jnp.int32)
    same_brick = (targets[:, None] == targets[None, :]) & (
        segment_ids[None, :] < segment_ids[:, None]
    )
    rank_within = jnp.sum(same_brick.astype(jnp.int32), axis=1)
    places = targets * capacity + rank_within
    slot_total = brick_count * capacity
    slot_ids = jnp.arange(slot_total, dtype=jnp.int32)
    slot_hits = places[None, :] == slot_ids[:, None]
    occupied = jnp.any(slot_hits, axis=1)
    source_index = jnp.max(jnp.where(slot_hits, segment_ids[None, :], 0), axis=1)

    def pack_slots(source):
        picked = jnp.take(source, source_index, axis=0)
        mask_shape = (slot_total,) + (1,) * (source.ndim - 1)
        packed = jnp.where(occupied.reshape(mask_shape), picked, jnp.zeros((), source.dtype))
        return packed.reshape((brick_count, capacity) + source.shape[1:])

    arrived, arrived_rows = (
        lax.all_to_all(
            pack_slots(spread_taps(values, kernels, kernel_taps)).astype(jnp.bfloat16),
            ("img", "freq"),
            split_axis=0,
            concat_axis=1,
            tiled=True,
        ).astype(jnp.float32),
        lax.all_to_all(
            pack_slots(voxel_rows), ("img", "freq"), split_axis=0, concat_axis=1, tiled=True
        ),
    )
    contributions = arrived.reshape(-1, 2, lane_count)
    row_count = BROWS
    row_member = (
        arrived_rows.reshape(-1)[None, :] == jnp.arange(row_count, dtype=jnp.int32)[:, None]
    )
    flat_terms = contributions.reshape(-1, 2 * lane_count)
    volume = jnp.dot(row_member.astype(jnp.float32), flat_terms, precision=lax.Precision.HIGHEST)
    volume = volume.reshape(row_count, 2, lane_count)
    return (own_rows, volume.transpose(1, 0, 2)[None])


def solution(mesh):
    in_specs = (
        P(None, "img", "freq"),
        P(None, "img", "freq"),
        P("freq"),
        P("img"),
        P("freq", "img", None, None),
        P("freq", "img", None),
        P("freq", "img", None),
        P(),
    )
    out_specs = (P("freq", "img"), P(("img", "freq"), None, None, None))
    return jax.shard_map(
        on_device, mesh=mesh, in_specs=in_specs, out_specs=out_specs, check_vma=False
    )
```

profile of v0, /device:TPU:1, one launch (start us, length us, event | category | flops | bytes accessed | tf_op | source)
XLA Modules:
  0.0 497.0 jit_solution(5238737698355671711)
XLA Ops:
  7.2 0.0 copy-start
  7.2 0.0 all-gather.3.cloned.1.call-start
  7.2 0.7 all-gather.3.cloned.1.call-update
  7.9 0.0 reduce-scatter.3.cloned.1.call-start
  8.0 87.0 %all-gather.3.cloned.1.call-done = bf16[2,896,2048]{2,1,0:T(8,128)(2,1)} async-done(((bf16[2,112,2048]{2,1,0:T(8,128)(2,1)}), bf16[2,896,2048]{2,1,0:T(8,128)(2,1)}) %all-gather.3.cloned.1.call-update) | async-done | bytes 7340048 | tf_op jit(solution)/shard_map/all_gather | solution.py:70
  95.0 10.1 %convert_element_type.24 = f32[2,896,2048]{2,1,0:T(8,128)} convert(bf16[2,896,2048]{2,1,0:T(8,128)(2,1)} %all-gather.3.cloned.1.call-done) | non-fusion elementwise | flops 3670016 | bytes 22020096 | tf_op jit(solution)/shard_map/convert_element_type | solution.py:70
  105.1 0.0 copy-done.4
  105.1 6.1 %fusion.9 = f32[896]{0:T(1024)S(1)} fusion(f32[2,896,2048]{2,1,0:T(8,128)} %convert_element_type.24, f32[2048]{0:T(1024)S(1)} %copy-done.4), kind=kLoop, calls=%fused_computation.18 | loop fusion | flops 9174144 | bytes 14691840 | tf_op jit(solution)/shard_map/reduce_sum | solution.py:72
  111.2 1.2 copy-done.1
  112.4 5.6 %multiply_convert_fusion = bf16[2,896,2048]{2,1,0:T(8,128)(2,1)} fusion(f32[2048]{0:T(1024)S(1)} %copy-done.4, bf16[2,896,2048]{2,1,0:T(8,128)(2,1)S(1)} %copy-done.1), kind=kLoop, calls=%fused_computation.9 | loop fusion | flops 11010048 | bytes 14688256 | tf_op jit(solution)/shard_map/convert_element_type | solution.py:71
  118.1 9.3 %fusion.10 = f32[896,1536]{1,0:T(8,128)S(1)} fusion(bf16[2,1536,2048]{2,1,0:T(8,128)(2,1)} %param.8, bf16[2,896,2048]{2,1,0:T(8,128)(2,1)} %multiply_convert_fusion), kind=kOutput, calls=%fused_computation.20 | convolution fusion | flops 5637144576 | bytes 15466496 | tf_op jit(solution)/shard_map/dot_general | solution.py:78
  127.4 9.7 %add_subtract_fusion = f32[896,1536]{1,0:T(8,128)} fusion(f32[896,1536]{1,0:T(8,128)S(1)} %fusion.10, bf16[2,1536,2048]{2,1,0:T(8,128)(2,1)} %param.8, bf16[2,896,2048]{2,1,0:T(8,128)(2,1)S(1)} %copy-done.2, f32[896]{0:T(1024)S(1)} %broadcast_multiply_fusion), kind=kOutput, calls=%fused_computation.28 | convolution fusion | flops 5639897088 | bytes 20975616 | tf_op jit(solution)/shard_map/dot_general | solution.py:75
  137.0 0.0 reduce-scatter.3.cloned.1.call-update
  137.0 0.0 all-gather.5.cloned.1.call-start
  137.1 83.8 %reduce-scatter.3.cloned.1.call-done = f32[56,1536]{1,0:T(8,128)} async-done(((f32[896,1536]{1,0:T(8,128)}), f32[56,1536]{1,0:T(8,128)}) %reduce-scatter.3.cloned.1.call-update) | async-done | bytes 344080 | tf_op jit(solution)/shard_map/reduce_scatter | solution.py:24
  220.9 0.0 all-gather.5.cloned.1.call-update
  220.9 0.5 reduce-scatter.5.cloned.1.call-start
  221.4 63.5 %all-gather.5.cloned.1.call-done = f32[896,1536]{1,0:T(8,128)} async-done(((f32[56,1536]{1,0:T(8,128)}), f32[896,1536]{1,0:T(8,128)}) %all-gather.5.cloned.1.call-update) | async-done | bytes 5505040 | tf_op jit(solution)/shard_map/all_gather | solution.py:25
  285.0 6.9 %fusion.40 = (f32[1536]{0:T(1024)S(1)}, f32[896,1536]{1,0:T(8,128)S(1)}) fusion(f32[896,1536]{1,0:T(8,128)} %all-gather.5.cloned.1.call-done, s32[1536]{0:T(1024)S(1)} %copy-done.8), kind=kLoop, calls=%fused_computation.72 | loop fusion | flops 17889792 | bytes 11022336 | tf_op jit(solution)/shard_map/reduce_max | solution.py:86
  291.9 0.8 fusion.23
  292.7 0.7 fusion.22
  293.4 2.4 copy-done.3
  295.8 0.3 slice-done.2
  296.1 13.5 %convolution_convert_fusion = bf16[896,2,2048]{2,0,1:T(8,128)(2,1)} fusion(bf16[2,1536,2048]{2,1,0:T(8,128)(2,1)S(1)} %bitcast.67, f32[896,1536]{1,0:T(8,128)S(1)} %fusion.22), kind=kOutput, calls=%fused_computation.36 | convolution fusion | flops 11279335424 | bytes 25427968 | tf_op jit(solution)/shard_map/oi,cif->ocf/dot_general | solution.py:94
  309.6 0.0 reduce-scatter.5.cloned.1.call-update
  309.6 0.7 copy-done.5
  310.3 0.1 copy.22
  310.4 0.1 reshape.147
  310.5 0.1 copy.23
  310.6 0.1 reshape.148
  310.7 1.2 convert_reduce_fusion
  311.9 4.3 select_reduce_fusion
  316.2 0.2 reduce_max.26
  316.4 0.1 fusion.39
  316.5 0.0 copy-start.7
  316.5 23.7 %gather_fusion = s32[4480]{0:T(1024)S(1)} fusion(s32[1792]{0:T(1024)S(1)} %reshape.148, s32[5120]{0:T(1024)S(1)} %pad_clamp_fusion), kind=kCustom, calls=%fused_computation | custom fusion | bytes 53760 | tf_op jit(solution)/shard_map/jit(_take)/gather | solution.py:126
  340.1 0.2 gather.13
  340.4 3.9 fusion.3
  344.3 0.2 reduce_or.12
  344.5 0.7 select_select_fusion
  345.2 6.5 %all-to-all-start = ((s32[128,1,35]{2,1,0:T(1,128)}), s32[128,1,35]{2,1,0:T(1,128)S(1)}, u32[]{:S(2)}, u32[]{:S(2)}) async-start(s32[128,1,35]{2,1,0:T(1,128)} %bitcast.5), calls=%async_computation.1 | async-start | bytes 131072 | tf_op jit(solution)/shard_map/all_to_all | solution.py:139
  351.6 0.2 reduce_max.28
  351.8 0.2 broadcast_in_dim.69
  352.1 0.1 copy.25
  352.2 0.1 eq.68
  352.3 0.6 fusion.37
  352.9 0.1 slice_reduce_fusion.3
  353.0 38.7 %reduce-scatter.5.cloned.1.call-done = bf16[112,2,2048]{2,0,1:T(8,128)(2,1)} async-done(((bf16[896,2,2048]{2,0,1:T(8,128)(2,1)}), bf16[112,2,2048]{2,0,1:T(8,128)(2,1)}) %reduce-scatter.5.cloned.1.call-update) | async-done | bytes 917520 | tf_op jit(solution)/shard_map/reduce_scatter | solution.py:93
  391.8 1.4 reshape.155
  393.2 0.3 copy.28
  393.5 1.4 copy.26
  394.9 14.6 %fusion.34 = bf16[1792,2,128]{2,1,0:T(2,128)(2,1)S(1)} fusion(f32[1792,2,128]{2,1,0:T(2,128)S(1)} %bitcast.63, f32[1792]{0:T(1024)S(1)} %get-tuple-element.3, f32[1792]{0:T(1024)S(1)} %get-tuple-element.4, f32[1792]{0:T(1024)S(1)} %get-tuple-element.5, f32[1792]{0:T(1024)S(1)} %get-tuple-element.2), kind=kLoop, calls=%fused_computation.52 | loop fusion | flops 3670016 | bytes 2781184 | tf_op jit(solution)/shard_map/add | solution.py:42
  409.5 14.4 %gather_fusion.1 = bf16[4480,2,128]{2,1,0:T(2,128)(2,1)S(1)} fusion(bf16[1792,2,128]{2,1,0:T(2,128)(2,1)S(1)} %fusion.34, s32[5120]{0:T(1024)S(1)} %pad_clamp_fusion), kind=kCustom, calls=%fused_computation.1 | custom fusion | bytes 4605440 | tf_op jit(solution)/shard_map/jit(_take)/gather | solution.py:126
  424.0 12.7 %select_convert_fusion = bf16[128,35,2,128]{3,2,1,0:T(2,128)(2,1)} fusion(bf16[128,35,2,128]{3,2,1,0:T(2,128)(2,1)S(1)} %bitcast.60, pred[128,35]{1,0:T(8,128)(4,1)S(1)} %compare_and_fusion, pred[128,35]{1,0:T(8,128)(4,1)S(1)} %broadcast_in_dim.69), kind=kLoop, calls=%fused_computation.39 | loop fusion | flops 2293760 | bytes 4596480 | tf_op jit(solution)/shard_map/convert_element_type | solution.py:133
  436.6 0.0 all-to-all-done
  436.6 7.1 %all-to-all-start.1 = ((bf16[128,35,2,128]{3,2,1,0:T(2,128)(2,1)}), bf16[128,35,2,128]{3,2,1,0:T(2,128)(2,1)S(1)}, u32[]{:S(2)}, u32[]{:S(2)}) async-start(bf16[128,35,2,128]{3,2,1,0:T(2,128)(2,1)} %select_convert_fusion), calls=%async_computation.3 | async-start | bytes 4587520 | tf_op jit(solution)/shard_map/all_to_all | solution.py:132
  443.7 0.5 broadcast.112
  444.2 0.8 reduce.13
  445.1 0.2 eq.64
  445.3 1.7 constant_dynamic-slice_fusion
  447.0 30.5 %all-to-all-done.1 = bf16[128,35,2,128]{3,2,1,0:T(2,128)(2,1)S(1)} async-done(((bf16[128,35,2,128]{3,2,1,0:T(2,128)(2,1)}), bf16[128,35,2,128]{3,2,1,0:T(2,128)(2,1)S(1)}, u32[]{:S(2)}, u32[]{:S(2)}) %all-to-all-start.1) | async-done | bytes 2293792 | tf_op jit(solution)/shard_map/all_to_all | solution.py:132
  477.5 1.7 copy.31
  479.2 3.0 copy.27
  482.2 8.1 %fusion.28 = f32[1,2,2000,128]{3,2,1,0:T(8,128)} fusion(bf16[2,128,4480]{2,1,0:T(8,128)(2,1)S(1)} %bitcast.65, s32[4480]{0:T(1024)S(1)} %eq.64), kind=kOutput, calls=%fused_computation.47 | convolution fusion | flops 4596480000 | bytes 4359680 | tf_op jit(solution)/shard_map/dot_general | solution.py:149
  (22 shorter events, 0.1 us)
Async XLA Ops:
  7.2 345.1 %copy-start = (f32[8,4]{0,1:T(4,128)S(1)}, f32[8,4]{0,1:T(4,128)}, u32[]{:S(2)}) copy-start(f32[8,4]{0,1:T(4,128)} %param.15) | copy-start | bytes 388
  7.2 87.8 %all-gather.3.cloned.1.call-start = ((), (), s32[]{:S(2)}) async-start(), calls=%async_computation.4 | async-start | bytes 8257536 | tf_op jit(solution)/shard_map/all_gather | solution.py:70
  7.9 97.2 %copy-start.4 = (f32[2048]{0:T(1024)S(1)}, f32[2048]{0:T(1024)}, u32[]{:S(2)}) copy-start(f32[2048]{0:T(1024)} %param.10) | copy-start | bytes 24580
  7.9 213.0 %reduce-scatter.3.cloned.1.call-start = ((), (), s32[]{:S(2)}) async-start(), calls=%async_computation.5 | async-start | bytes 5849088 | tf_op jit(solution)/shard_map/reduce_scatter | solution.py:24
  105.1 7.3 %copy-start.1 = (bf16[2,896,2048]{2,1,0:T(8,128)(2,1)S(1)}, bf16[2,896,2048]{2,1,0:T(8,128)(2,1)}, u32[]{:S(2)}) copy-start(bf16[2,896,2048]{2,1,0:T(8,128)(2,1)} %all-gather.3.cloned.1.call-done) | copy-start | bytes 22020100
  118.1 9.3 %copy-start.2 = (bf16[2,896,2048]{2,1,0:T(8,128)(2,1)S(1)}, bf16[2,896,2048]{2,1,0:T(8,128)(2,1)}, u32[]{:S(2)}) copy-start(bf16[2,896,2048]{2,1,0:T(8,128)(2,1)} %multiply_convert_fusion) | copy-start | bytes 22020100
  137.0 148.0 %copy-start.8 = (s32[1536]{0:T(1024)S(1)}, s32[1536]{0:T(1024)}, u32[]{:S(2)}) copy-start(s32[1536]{0:T(1024)} %param.11) | copy-start | bytes 18436
  137.0 147.9 %all-gather.5.cloned.1.call-start = ((), (), s32[]{:S(2)}) async-start(), calls=%async_computation.6 | async-start | bytes 5849088 | tf_op jit(solution)/shard_map/all_gather | solution.py:25
  220.9 170.9 %reduce-scatter.5.cloned.1.call-start = ((), (), s32[]{:S(2)}) async-start(), calls=%async_computation.7 | async-start | bytes 8257536 | tf_op jit(solution)/shard_map/reduce_scatter | solution.py:93
  285.0 10.9 %slice-start = ((s8[12582912]{0:T(1024)(128)(4,1)}), s8[4194304]{0:T(1024)(128)(4,1)S(1)}, s32[]{:S(2)}) async-start(s8[12582912]{0:T(1024)(128)(4,1)} %bitcast.66), calls=%async_computation.8 | async-start | bytes 8388608
  285.0 10.9 %slice-start.1 = ((s8[12582912]{0:T(1024)(128)(4,1)}), s8[4194304]{0:T(1024)(128)(4,1)S(1)}, s32[]{:S(2)}) async-start(s8[12582912]{0:T(1024)(128)(4,1)} %bitcast.66), calls=%async_computation.9 | async-start | bytes 8388608
  292.7 3.4 slice-start.2
  293.4 2.4 copy-start.3
  309.6 0.7 copy-start.5
  309.6 0.9 copy-start.6
  316.5 35.6 %copy-start.7 = (s32[1,112,16]{1,2,0:T(8,128)S(1)}, s32[1,112,16]{1,2,0:T(8,128)}, u32[]{:S(2)}) copy-start(s32[1,112,16]{1,2,0:T(8,128)} %param.14) | copy-start | bytes 21508
  345.2 91.5 %all-to-all-start = ((s32[128,1,35]{2,1,0:T(1,128)}), s32[128,1,35]{2,1,0:T(1,128)S(1)}, u32[]{:S(2)}, u32[]{:S(2)}) async-start(s32[128,1,35]{2,1,0:T(1,128)} %bitcast.5), calls=%async_computation.1 | async-start | bytes 131072 | tf_op jit(solution)/shard_map/all_to_all | solution.py:139
  436.6 40.9 %all-to-all-start.1 = ((bf16[128,35,2,128]{3,2,1,0:T(2,128)(2,1)}), bf16[128,35,2,128]{3,2,1,0:T(2,128)(2,1)S(1)}, u32[]{:S(2)}, u32[]{:S(2)}) async-start(bf16[128,35,2,128]{3,2,1,0:T(2,128)(2,1)} %select_convert_fusion), calls=%async_computation.3 | async-start | bytes 4587520 | tf_op jit(solution)/shard_map/all_to_all | solution.py:132
Sparse Core Ops, SparseCore 0:
  9.7 85.2 all-gather.2
  137.2 83.6 reduce-scatter.2
  223.6 61.3 all-gather.4
  309.8 81.9 reduce-scatter.4
where the time goes:
time: 504 us; the launch traced here: 497 us
  waiting for transfers between devices  304 us (60%)
  other arithmetic  69.9 us (14%)
  local copies, waits for them, and re-layouts  53.2 us (11%)
  matrix products  41.2 us (8%)
  between operations  14.3 us (3%)
  starting transfers between devices  14.2 us (3%)
    all_gather x1, waiting for transfers between devices, on_device(): lax.all_gather(references, 'img', axis=1, tiled=True).astype(jnp.float32)  87 us
    reduce_scatter x1, waiting for transfers between devices, sum_by_parts(): own = lax.psum_scatter(padded, axis, scatter_dimension=0, tiled=True)  83.8 us
    all_gather x1, waiting for transfers between devices, sum_by_parts(): whole = lax.all_gather(own, axis, axis=0, tiled=True)  63.5 us
    reduce_scatter x1, waiting for transfers between devices, on_device(): lax.psum_scatter(jnp.einsum('oi,cif->ocf', rounded, images, preferred_ele...  38.7 us
    gather x3, local copies, waits for them, and re-layouts, pack_slots(): picked = jnp.take(source, source_index, axis=0)  38.3 us
    all_to_all x1, waiting for transfers between devices, on_device(): lax.all_to_all(pack_slots(spread_taps(values, kernels, kernel_taps)).asty...  30.5 us
    add x1, other arithmetic, spread_taps(): result + factors[:, tap_index, None, None] * padded[:, :, first_lane:firs...  14.6 us
    dot_general x1, matrix products, on_device(): jnp.einsum('oi,cif->ocf', rounded, images, preferred_element_type=jnp.flo...  13.5 us
  transfers between devices with their start and end apart: 6, of which 5 were waited for; matrix products, arithmetic and copies ran while one was open for 17% of the time, Pallas kernels for 0%

commit v1 on v0

v1 whole, which is shorter than its diff:
```python
import jax
import jax.numpy as jnp
from jax import lax
from jax.sharding import PartitionSpec as P

BROWS = 2000
KEPT = 240
COARSE = 128
FINE = (64, 32, 16, 8)


tempering = 0.5
masked_logit = -1e30
contract_last = (((1,), (1,)), ((), ()))


def window_parts(prior_orient, orient_count):
    start = (prior_orient - orient_count // 8) % orient_count
    return start // COARSE, start % COARSE


def to_windows(scores, prior_orient):
    orient_count = scores.shape[0]
    coarse, fine = window_parts(prior_orient, orient_count)
    rows = KEPT + sum(FINE)
    ring = jnp.concatenate([scores, scores[: rows - COARSE]], axis=0)
    kept = ring[:rows]
    for block in range(1, orient_count // COARSE):
        kept = jnp.where((coarse == block)[None], ring[block * COARSE : block * COARSE + rows], kept)
    for step in FINE:
        rows -= step
        kept = jnp.where(((fine // step) % 2 == 1)[None], kept[step : step + rows], kept[:rows])
    return kept


def from_windows(kept, prior_orient, orient_count):
    coarse, fine = window_parts(prior_orient, orient_count)
    for step in FINE[::-1]:
        pad = jnp.zeros((step, kept.shape[1]), kept.dtype)
        kept = jnp.where(
            ((fine // step) % 2 == 1)[None],
            jnp.concatenate([pad, kept], axis=0),
            jnp.concatenate([kept, pad], axis=0),
        )
    kept = jnp.pad(kept, ((0, -kept.shape[0] % COARSE), (0, 0)))
    blocks = orient_count // COARSE
    parts = []
    for block in range(blocks):
        part = jnp.zeros((COARSE, kept.shape[1]), kept.dtype)
        for piece in range(kept.shape[0] // COARSE):
            part = jnp.where(
                (coarse == (block - piece) % blocks)[None],
                kept[piece * COARSE : (piece + 1) * COARSE],
                part,
            )
        parts.append(part)
    return jnp.concatenate(parts, axis=0)


def window_softmax(scores, prior_orient, orient_count):
    fine = window_parts(prior_orient, orient_count)[1] % FINE[-1]
    position = jnp.arange(scores.shape[1], dtype=jnp.int32)[None, :]
    inside = (position >= fine[:, None]) & (position <= fine[:, None] + 2 * (orient_count // 8))
    logits = jnp.where(inside, tempering * scores, masked_logit)
    raised = jnp.where(inside, jnp.exp(logits - jnp.max(logits, axis=1, keepdims=True)), 0.0)
    return raised / jnp.sum(raised, axis=1, keepdims=True)


def spread_taps(values, kernels, kernel_taps):
    phases, tap_count = kernel_taps.shape
    member = (kernels[:, None] == jnp.arange(phases, dtype=jnp.int32)[None, :]).astype(
        kernel_taps.dtype
    )
    factors = jnp.dot(member, kernel_taps, precision=lax.Precision.HIGHEST)
    padded = jnp.pad(values, ((0, 0), (0, 0), (tap_count - 2, 1)))
    lane_count = values.shape[2]
    result = jnp.zeros(values.shape, values.dtype)
    for tap_index in range(tap_count):
        first_lane = tap_count - 1 - tap_index
        result = (
            result
            + factors[None, :, tap_index, None] * padded[:, :, first_lane : first_lane + lane_count]
        )
    return result


def on_device(
    images,
    references,
    noise_weight,
    prior_orient,
    segment_brick,
    segment_row,
    segment_kernel,
    kernel_taps,
):
    image_groups = lax.axis_size("img")
    freq_groups = lax.axis_size("freq")
    local_orients = references.shape[1]
    orient_count = local_orients * image_groups
    share_rows = orient_count // freq_groups
    share_images = images.shape[1] // freq_groups
    unpacked = lax.all_gather(references, "img", axis=1, tiled=True).astype(jnp.float32)
    weighted = (noise_weight * unpacked).astype(jnp.bfloat16)
    energies = jnp.sum(
        noise_weight * (unpacked[0] * unpacked[0] + unpacked[1] * unpacked[1]), axis=1
    )
    products = lax.dot_general(
        weighted[0], images[0], contract_last, preferred_element_type=jnp.float32
    )
    products = products + lax.dot_general(
        weighted[1], images[1], contract_last, preferred_element_type=jnp.float32
    )
    partial_scores = products - 0.5 * energies[:, None]
    windows = to_windows(partial_scores, prior_orient).T
    scores = lax.psum_scatter(windows, "freq", scatter_dimension=0, tiled=True)
    own_prior = lax.dynamic_slice_in_dim(
        prior_orient, lax.axis_index("freq") * share_images, share_images, 0
    )
    kept = window_softmax(scores, own_prior, orient_count).astype(jnp.bfloat16)
    kept = lax.all_gather(kept, "freq", axis=0, tiled=True).T
    rounded = from_windows(kept, prior_orient, orient_count)
    own_rows = lax.dynamic_slice_in_dim(
        rounded, lax.axis_index("freq") * share_rows, share_rows, 0
    ).astype(jnp.float32)
    weighted_sums = lax.psum_scatter(
        jnp.einsum("oi,cif->cof", rounded, images, preferred_element_type=jnp.float32).astype(
            jnp.bfloat16
        ),
        "img",
        scatter_dimension=1,
        tiled=True,
    ).astype(jnp.float32)
    segment_blocks = segment_row.shape[2]
    lane_count = images.shape[2] // segment_blocks
    local_segments = local_orients * segment_blocks
    values = weighted_sums.reshape(2, local_orients, segment_blocks, lane_count)
    values = values.transpose(0, 2, 1, 3).reshape(2, local_segments, lane_count)
    targets = segment_brick.reshape(local_orients, segment_blocks).T.reshape(-1)
    voxel_rows = segment_row.reshape(local_orients, segment_blocks).T.reshape(-1)
    kernels = segment_kernel.reshape(local_orients, segment_blocks).T.reshape(-1)
    brick_count = image_groups * freq_groups
    capacity = max(2, 5 * local_segments // (2 * brick_count))
    segment_ids = jnp.arange(local_segments, dtype=jnp.int32)
    same_brick = (targets[:, None] == targets[None, :]) & (
        segment_ids[None, :] < segment_ids[:, None]
    )
    rank_within = jnp.sum(same_brick.astype(jnp.int32), axis=1)
    places = targets * capacity + rank_within
    slot_total = brick_count * capacity
    slot_ids = jnp.arange(slot_total, dtype=jnp.int32)
    slot_hits = places[None, :] == slot_ids[:, None]
    packed_rows = jnp.sum(jnp.where(slot_hits, voxel_rows[None, :], 0), axis=1)
    contributions = spread_taps(values, kernels, kernel_taps).astype(jnp.bfloat16)
    hits = slot_hits.astype(jnp.bfloat16)
    packed = jnp.stack(
        [jnp.dot(hits, part, preferred_element_type=jnp.float32) for part in contributions], axis=1
    ).astype(jnp.bfloat16)
    exchange = lambda lines: lax.all_to_all(
        lines.reshape(brick_count, capacity, -1),
        ("img", "freq"),
        split_axis=0,
        concat_axis=0,
        tiled=True,
    )
    arrived_rows = exchange(packed_rows).reshape(-1)
    arrived = exchange(packed).reshape(slot_total, 2 * lane_count)
    row_member = arrived_rows[None, :] == jnp.arange(BROWS, dtype=jnp.int32)[:, None]
    volume = jnp.stack(
        [
            jnp.dot(
                row_member.astype(jnp.bfloat16),
                arrived[:, part * lane_count : (part + 1) * lane_count],
                preferred_element_type=jnp.float32,
            )
            for part in range(2)
        ]
    )
    return (own_rows, volume[None])


def solution(mesh):
    in_specs = (
        P(None, "img", "freq"),
        P(None, "img", "freq"),
        P("freq"),
        P("img"),
        P("freq", "img", None, None),
        P("freq", "img", None),
        P("freq", "img", None),
        P(),
    )
    out_specs = (P("freq", "img"), P(("img", "freq"), None, None, None))
    return jax.shard_map(
        on_device, mesh=mesh, in_specs=in_specs, out_specs=out_specs, check_vma=False
    )
```

time: 504 us -> 463 us (0.919)
  waiting for transfers between devices: 304 us -> 255 us
  blocking collectives: 0 us -> 26.3 us
  local copies, waits for them, and re-layouts: 53.2 us -> 34.4 us
  other arithmetic: 69.9 us -> 53.7 us
  matrix products: 41.2 us -> 56.6 us
    all_gather x1 -> x0, waiting for transfers between devices: 63.5 us -> none  [sum_by_parts(): whole = lax.all_gather(own, axis, axis=0, tiled=True)]
    gather x3 -> x0, local copies, waits for them, and re-layouts: 38.3 us -> none  [pack_slots(): picked = jnp.take(source, source_index, axis=0)]
    all_gather x0 -> x1, blocking collectives: none -> 26.3 us  [on_device(): kept = lax.all_gather(kept, 'freq', axis=0, tiled=True).T]
    another operation x0 -> x1, local copies, waits for them, and re-layouts: none -> 19.5 us  [on_device(): jnp.stack([jnp.dot(hits, part, preferred_element_type=jnp.float32) for pa...]
    dot_general x2 -> x5, matrix products: 21.6 us -> 38.6 us  [the longest x2 13.9 us: on_device(): jnp.dot(row_member.astype(jnp.bfloat16), arrived[:, part * lane_count:(pa...]
    add x1, other arithmetic: 14.6 us -> 0.8 us  [window_softmax(): fine[:, None] + 2 * (orient_count // 8)]
    reduce_scatter x2, waiting for transfers between devices: 123 us -> 134 us  [the longest x1 68.7 us: on_device(): lax.psum_scatter(jnp.einsum('oi,cif->cof', rounded, images, preferred_ele...]
    reduce_max x2 -> x1, other arithmetic: 11.2 us -> 1.09 us  [window_softmax(): jnp.max(logits, axis=1, keepdims=True)]
  transfers between devices with their start and end apart: 6 -> 5, of which waited for: 5 -> 4; matrix products, arithmetic and copies ran while one was open for 17% -> 13% of each run, Pallas kernels for 0% -> 0%
where the time goes in v1:
time: 463 us; the launch traced here: 454 us
  waiting for transfers between devices  255 us (55%)
  matrix products  56.6 us (12%)
  other arithmetic  53.7 us (12%)
  local copies, waits for them, and re-layouts  34.4 us (7%)
  blocking collectives  26.3 us (6%)
  between operations  14.5 us (3%)
  starting transfers between devices  13.1 us (3%)
    all_gather x1, waiting for transfers between devices, on_device(): lax.all_gather(references, 'img', axis=1, tiled=True).astype(jnp.float32)  86.2 us
    reduce_scatter x1, waiting for transfers between devices, on_device(): lax.psum_scatter(jnp.einsum('oi,cif->cof', rounded, images, preferred_ele...  68.7 us
    reduce_scatter x1, waiting for transfers between devices, on_device(): scores = lax.psum_scatter(windows, 'freq', scatter_dimension=0, tiled=True)  65 us
    all_to_all x2, waiting for transfers between devices, on_device(): lax.all_to_all(lines.reshape(brick_count, capacity, -1), ('img', 'freq'),...  34.8 us
    all_gather x1, blocking collectives, on_device(): kept = lax.all_gather(kept, 'freq', axis=0, tiled=True).T  26.3 us
    another operation x1, local copies, waits for them, and re-layouts, on_device(): jnp.stack([jnp.dot(hits, part, preferred_element_type=jnp.float32) for pa...  19.5 us
    dot_general x2, matrix products, on_device(): jnp.dot(row_member.astype(jnp.bfloat16), arrived[:, part * lane_count:(pa...  13.9 us
    dot_general x1, matrix products, on_device(): jnp.einsum('oi,cif->cof', rounded, images, preferred_element_type=jnp.flo...  13.3 us
  transfers between devices with their start and end apart: 5, of which 4 were waited for; matrix products, arithmetic and copies ran while one was open for 13% of the time, Pallas kernels for 0%

profile of v1, /device:TPU:1, one launch (start us, length us, event | category | flops | bytes accessed | tf_op | source)
XLA Modules:
  0.0 454.1 jit_solution(1847253555957829692)
XLA Ops:
  7.2 0.7 all-gather.2.cloned.1.call-update
  8.0 0.7 fusion.59
  8.8 86.2 %all-gather.2.cloned.1.call-done = bf16[2,896,2048]{2,1,0:T(8,128)(2,1)} async-done(((bf16[2,112,2048]{2,1,0:T(8,128)(2,1)}), bf16[2,896,2048]{2,1,0:T(8,128)(2,1)}) %all-gather.2.cloned.1.call-update) | async-done | bytes 7340048 | tf_op jit(solution)/shard_map/all_gather | solution.py:103
  95.0 10.1 %convert_element_type.38 = f32[2,896,2048]{2,1,0:T(8,128)} convert(bf16[2,896,2048]{2,1,0:T(8,128)(2,1)} %all-gather.2.cloned.1.call-done) | non-fusion elementwise | flops 3670016 | bytes 22020096 | tf_op jit(solution)/shard_map/convert_element_type | solution.py:103
  105.1 6.1 %fusion.12 = f32[896]{0:T(1024)S(1)} fusion(f32[2,896,2048]{2,1,0:T(8,128)} %convert_element_type.38, f32[2048]{0:T(1024)S(1)} %copy-done.5), kind=kLoop, calls=%fused_computation.19 | loop fusion | flops 9174144 | bytes 14691840 | tf_op jit(solution)/shard_map/reduce_sum | solution.py:105
  111.2 1.2 copy-done.1
  112.4 5.6 %multiply_convert_fusion = bf16[2,896,2048]{2,1,0:T(8,128)(2,1)} fusion(f32[2048]{0:T(1024)S(1)} %copy-done.5, bf16[2,896,2048]{2,1,0:T(8,128)(2,1)S(1)} %copy-done.1), kind=kLoop, calls=%fused_computation.11 | loop fusion | flops 11010048 | bytes 14688256 | tf_op jit(solution)/shard_map/convert_element_type | solution.py:104
  118.1 9.3 %fusion.13 = f32[896,1536]{1,0:T(8,128)S(1)} fusion(bf16[2,1536,2048]{2,1,0:T(8,128)(2,1)} %param.8, bf16[2,896,2048]{2,1,0:T(8,128)(2,1)} %multiply_convert_fusion), kind=kOutput, calls=%fused_computation.22 | convolution fusion | flops 5637144576 | bytes 15466496 | tf_op jit(solution)/shard_map/dot_general | solution.py:111
  127.3 8.1 %add_subtract_fusion = f32[896,1536]{1,0:T(8,128)S(1)} fusion(f32[896,1536]{1,0:T(8,128)S(1)} %fusion.13, bf16[2,1536,2048]{2,1,0:T(8,128)(2,1)} %param.8, bf16[2,896,2048]{2,1,0:T(8,128)(2,1)S(1)} %copy-done.2, f32[896]{0:T(1024)S(1)} %broadcast_multiply_fusion), kind=kOutput, calls=%fused_computation.32 | convolution fusion | flops 5639897088 | bytes 20975616 | tf_op jit(solution)/shard_map/dot_general | solution.py:108
  135.4 0.1 slice.163
  135.5 1.9 fusion.32
  137.5 0.2 slice_select_fusion.1
  137.6 0.1 slice_select_fusion.2
  137.8 0.1 slice_select_fusion.3
  137.9 0.1 fusion.40
  138.0 1.6 copy.27
  139.7 0.8 broadcast_add_fusion
  140.5 65.0 %reduce-scatter.7.cloned.1.call-done = f32[96,240]{1,0:T(8,128)} async-done(((f32[1536,240]{1,0:T(8,128)}), f32[96,240]{1,0:T(8,128)}) %reduce-scatter.7.cloned.1.call-update) | async-done | bytes 92176 | tf_op jit(solution)/shard_map/reduce_scatter | solution.py:116
  205.6 1.1 fusion.46
  206.6 1.1 fusion.47
  207.8 1.0 divide_convert_fusion
  208.8 26.3 %all_gather.7 = bf16[1536,240]{1,0:T(8,128)(2,1)S(1)} all-gather(bf16[96,240]{1,0:T(8,128)(2,1)S(1)} %divide_convert_fusion), channel_id=1, replica_groups=mesh['img'=8,'freq'=16] {'freq'}, dimensions={0}, use_global_device_ids=true | all-gather | bytes 783360 | tf_op jit(solution)/shard_map/all_gather | solution.py:121
  235.1 0.3 copy.23
  235.4 0.1 pad_select_fusion.3
  235.6 0.1 pad_select_fusion.2
  235.7 0.1 pad_select_fusion.1
  235.9 0.2 pad_select_fusion
  236.1 0.2 select_dynamic-update-slice_fusion.6
  236.2 0.2 select_dynamic-update-slice_fusion.5
  236.4 0.2 select_dynamic-update-slice_fusion.4
  236.6 0.2 select_dynamic-update-slice_fusion.3
  236.8 0.2 select_dynamic-update-slice_fusion.2
  237.0 0.2 select_dynamic-update-slice_fusion.1
  237.2 0.2 select_dynamic-update-slice_fusion
  237.4 1.6 copy-done.4
  239.0 1.1 slice-done.1
  240.0 1.3 slice-done.2
  241.3 13.3 %convert_bitcast_fusion = bf16[2,896,2048]{2,1,0:T(8,128)(2,1)} fusion(bf16[2,1536,2048]{2,1,0:T(8,128)(2,1)S(1)} %bitcast.72, bf16[896,1536]{1,0:T(8,128)(2,1)S(1)} %select_dynamic-update-slice_fusion), kind=kOutput, calls=%fused_computation.21 | convolution fusion | flops 11277959168 | bytes 22675456 | tf_op jit(solution)/shard_map/oi,cif->cof/dot_general | solution.py:127
  254.7 0.7 copy-done.6
  255.4 0.1 broadcast_in_dim.277
  255.5 1.2 convert_reduce_fusion
  256.7 3.3 select_reduce_fusion
  260.0 0.8 reshape.80
  260.8 6.2 %all-to-all-start = ((s32[128,35,1]{1,2,0:T(1,128)}), s32[128,35,1]{1,2,0:T(1,128)S(1)}, u32[]{:S(2)}, u32[]{:S(2)}) async-start(s32[128,35,1]{1,2,0:T(1,128)} %bitcast.11), calls=%async_computation | async-start | bytes 131072 | tf_op jit(solution)/shard_map/all_to_all | solution.py:159
  267.1 0.6 fusion.43
  267.8 0.1 slice_reduce_fusion.3
  267.9 68.7 %reduce-scatter.5.cloned.1.call-done = bf16[2,112,2048]{2,1,0:T(8,128)(2,1)} async-done(((bf16[2,896,2048]{2,1,0:T(8,128)(2,1)}), bf16[2,112,2048]{2,1,0:T(8,128)(2,1)}) %reduce-scatter.5.cloned.1.call-update) | async-done | bytes 917520 | tf_op jit(solution)/shard_map/reduce_scatter | solution.py:126
  336.6 1.3 copy_bitcast_fusion
  337.9 12.8 %fusion.37 = bf16[2,1792,128]{2,1,0:T(8,128)(2,1)S(1)} fusion(f32[2,1792,128]{2,1,0:T(8,128)S(1)} %bitcast.66, f32[1792]{0:T(1024)S(1)} %get-tuple-element.3, f32[1792]{0:T(1024)S(1)} %get-tuple-element.4, f32[1792]{0:T(1024)S(1)} %get-tuple-element.5, f32[1792]{0:T(1024)S(1)} %get-tuple-element.2), kind=kLoop, calls=%fused_computation.54 | loop fusion | flops 3670016 | bytes 2781184 | tf_op jit(solution)/shard_map/convert_element_type | solution.py:154
  350.7 5.7 %fusion.21 = bf16[4480,1,128]{2,0,1:T(8,128)(2,1)S(1)} fusion(s32[1792]{0:T(1024)S(1)} %multiply_add_fusion, bf16[2,1792,128]{2,1,0:T(8,128)(2,1)S(1)} %fusion.37), kind=kOutput, calls=%fused_computation.30 | convolution fusion | flops 2063810560 | bytes 1613824 | tf_op jit(solution)/shard_map/dot_general | solution.py:157
  356.4 5.7 %fusion.22 = bf16[4480,1,128]{2,0,1:T(8,128)(2,1)S(1)} fusion(s32[1792]{0:T(1024)S(1)} %multiply_add_fusion, bf16[2,1792,128]{2,1,0:T(8,128)(2,1)S(1)} %fusion.37), kind=kOutput, calls=%fused_computation.31 | convolution fusion | flops 2063810560 | bytes 1613824 | tf_op jit(solution)/shard_map/dot_general | solution.py:157
  362.1 0.2 pad_maximum_fusion
  362.3 19.5 %copy.26 = bf16[4480,2,128]{2,1,0:T(2,128)(2,1)S(1)} copy(bf16[4480,2,128]{2,0,1:T(8,128)(2,1)S(1)} %pad_maximum_fusion) | data formatting | bytes 4587520 | tf_op jit(solution)/shard_map/stack | solution.py:156
  381.8 2.8 convert_element_type.46
  384.6 6.8 %all-to-all-start.1 = ((bf16[128,35,256]{2,1,0:T(8,128)(2,1)}), bf16[128,35,256]{2,1,0:T(8,128)(2,1)S(1)}, u32[]{:S(2)}, u32[]{:S(2)}) async-start(bf16[128,35,256]{2,1,0:T(8,128)(2,1)} %convert_element_type.46), calls=%async_computation.2 | async-start | bytes 5242880 | tf_op jit(solution)/shard_map/all_to_all | solution.py:159
  391.4 0.5 broadcast.153
  391.9 0.8 reduce.11
  392.7 0.2 eq.147
  392.9 1.7 dynamic-slice_convert_fusion
  394.6 34.8 %all-to-all-done.1 = bf16[128,35,256]{2,1,0:T(8,128)(2,1)S(1)} async-done(((bf16[128,35,256]{2,1,0:T(8,128)(2,1)}), bf16[128,35,256]{2,1,0:T(8,128)(2,1)S(1)}, u32[]{:S(2)}, u32[]{:S(2)}) %all-to-all-start.1) | async-done | bytes 2293792 | tf_op jit(solution)/shard_map/all_to_all | solution.py:159
  429.4 2.4 reshape.85
  431.8 7.7 %fusion.26 = f32[1,2000,128]{2,1,0:T(8,128)S(1)} fusion(s32[4480]{0:T(1024)S(1)} %eq.147, bf16[4480,256]{1,0:T(8,128)(2,1)} %reshape.85), kind=kOutput, calls=%fused_computation.39 | convolution fusion | flops 2302720000 | bytes 2188800 | tf_op jit(solution)/shard_map/dot_general | solution.py:171
  439.5 6.2 %fusion.27 = f32[1,2000,128]{2,1,0:T(8,128)S(1)} fusion(s32[4480]{0:T(1024)S(1)} %eq.147, bf16[4480,256]{1,0:T(8,128)(2,1)S(1)} %copy-done.3), kind=kOutput, calls=%fused_computation.40 | convolution fusion | flops 2302720000 | bytes 2191360 | tf_op jit(solution)/shard_map/dot_general | solution.py:171
  445.7 1.4 maximum_bitcast_fusion
  (32 shorter events, 0.4 us)
Async XLA Ops:
  7.2 259.9 %copy-start = (f32[8,4]{0,1:T(4,128)S(1)}, f32[8,4]{0,1:T(4,128)}, u32[]{:S(2)}) copy-start(f32[8,4]{0,1:T(4,128)} %param.15) | copy-start | bytes 388
  7.2 87.8 %all-gather.2.cloned.1.call-start = ((), (), s32[]{:S(2)}) async-start(), calls=%async_computation.4 | async-start | bytes 8257536 | tf_op jit(solution)/shard_map/all_gather | solution.py:103
  7.9 197.6 %reduce-scatter.7.cloned.1.call-start = ((), (), s32[]{:S(2)}) async-start(), calls=%async_computation.6 | async-start | bytes 1671168 | tf_op jit(solution)/shard_map/reduce_scatter | solution.py:116
  8.8 96.3 %copy-start.5 = (f32[2048]{0:T(1024)S(1)}, f32[2048]{0:T(1024)}, u32[]{:S(2)}) copy-start(f32[2048]{0:T(1024)} %param.10) | copy-start | bytes 24580
  105.1 7.3 %copy-start.1 = (bf16[2,896,2048]{2,1,0:T(8,128)(2,1)S(1)}, bf16[2,896,2048]{2,1,0:T(8,128)(2,1)}, u32[]{:S(2)}) copy-start(bf16[2,896,2048]{2,1,0:T(8,128)(2,1)} %all-gather.2.cloned.1.call-done) | copy-start | bytes 22020100
  118.1 9.3 %copy-start.2 = (bf16[2,896,2048]{2,1,0:T(8,128)(2,1)S(1)}, bf16[2,896,2048]{2,1,0:T(8,128)(2,1)}, u32[]{:S(2)}) copy-start(bf16[2,896,2048]{2,1,0:T(8,128)(2,1)} %multiply_convert_fusion) | copy-start | bytes 22020100
  139.7 196.9 %reduce-scatter.5.cloned.1.call-start = ((), (), s32[]{:S(2)}) async-start(), calls=%async_computation.5 | async-start | bytes 8257536 | tf_op jit(solution)/shard_map/reduce_scatter | solution.py:126
  235.4 3.5 slice-start
  236.0 4.0 slice-start.1
  236.6 4.7 %slice-start.2 = ((s8[12582912]{0:T(1024)(128)(4,1)}), s8[4194304]{0:T(1024)(128)(4,1)S(1)}, s32[]{:S(2)}) async-start(s8[12582912]{0:T(1024)(128)(4,1)} %bitcast.71), calls=%async_computation.9 | async-start | bytes 8388608
  237.4 1.6 copy-start.4
  254.6 0.7 copy-start.6
  254.6 0.8 copy-start.7
  254.6 12.4 %copy-start.8 = (s32[1,112,16]{1,2,0:T(8,128)S(1)}, s32[1,112,16]{1,2,0:T(8,128)}, u32[]{:S(2)}) copy-start(s32[1,112,16]{1,2,0:T(8,128)} %param.14) | copy-start | bytes 21508
  260.8 123.8 %all-to-all-start = ((s32[128,35,1]{1,2,0:T(1,128)}), s32[128,35,1]{1,2,0:T(1,128)S(1)}, u32[]{:S(2)}, u32[]{:S(2)}) async-start(s32[128,35,1]{1,2,0:T(1,128)} %bitcast.11), calls=%async_computation | async-start | bytes 131072 | tf_op jit(solution)/shard_map/all_to_all | solution.py:159
  384.6 44.8 %all-to-all-start.1 = ((bf16[128,35,256]{2,1,0:T(8,128)(2,1)}), bf16[128,35,256]{2,1,0:T(8,128)(2,1)S(1)}, u32[]{:S(2)}, u32[]{:S(2)}) async-start(bf16[128,35,256]{2,1,0:T(8,128)(2,1)} %convert_element_type.46), calls=%async_computation.2 | async-start | bytes 5242880 | tf_op jit(solution)/shard_map/all_to_all | solution.py:159
  431.8 7.7 %copy-start.3 = (bf16[4480,256]{1,0:T(8,128)(2,1)S(1)}, bf16[4480,256]{1,0:T(8,128)(2,1)}, u32[]{:S(2)}) copy-start(bf16[4480,256]{1,0:T(8,128)(2,1)} %reshape.85) | copy-start | bytes 6881284
Sparse Core Ops, SparseCore 0:
  9.7 85.2 all-gather.1
  139.8 65.7 reduce-scatter.6
  254.8 81.7 reduce-scatter.4

commit v2 on v1

--- a/solution.py
+++ b/solution.py
@@ -1,10 +1,18 @@
 import jax
 import jax.numpy as jnp
 from jax import lax
+from jax.experimental import pallas as pl
+from jax.experimental.pallas import tpu as pltpu
 from jax.sharding import PartitionSpec as P
 
+MESH = pl.DeviceIdType.MESH
+VMEM = pltpu.VMEM
+DMA = pltpu.SemaphoreType.DMA
+VMEM_BYTES = 60 * 1024 * 1024
+RING = 4
+
 BROWS = 2000
-KEPT = 240
+KEPT = 256
 COARSE = 128
 FINE = (64, 32, 16, 8)
 
@@ -57,13 +65,369 @@
     return jnp.concatenate(parts, axis=0)
 
 
-def window_softmax(scores, prior_orient, orient_count):
-    fine = window_parts(prior_orient, orient_count)[1] % FINE[-1]
-    position = jnp.arange(scores.shape[1], dtype=jnp.int32)[None, :]
-    inside = (position >= fine[:, None]) & (position <= fine[:, None] + 2 * (orient_count // 8))
+def img_neighbours():
+    me = lax.axis_index("img")
+    z, x = me // RING, me % RING
+    at = lambda other, shift: (z + other) % 2 * RING + (x + shift) % RING
+    return at
+
+
+def greet(axis, others):
+    barrier = pltpu.get_barrier_semaphore()
+    for other in others:
+        pl.semaphore_signal(barrier, inc=1, device_id={axis: other}, device_id_type=MESH)
+    pl.semaphore_wait(barrier, len(others))
+
+
+def score_kernel(
+    refs_ref, noise_ref, images_hbm, out_ref, images, gathered, weighted, energy,
+    load_sem, own_sem, send_sem, recv_sem,
+):
+    at = img_neighbours()
+    rows = refs_ref.shape[1]
+    load = pltpu.make_async_copy(images_hbm, images, load_sem)
+    load.start()
+    own = pltpu.make_async_copy(refs_ref, gathered.at[at(0, 0)], own_sem)
+    own.start()
+    greet("img", [at(0, 1), at(0, 3), at(1, 0)])
+    own.wait()
+
+    def send(number, shard, part, target):
+        copy = pltpu.make_async_remote_copy(
+            src_ref=gathered.at[shard, part],
+            dst_ref=gathered.at[shard, part],
+            send_sem=send_sem.at[number],
+            recv_sem=recv_sem.at[number],
+            device_id={"img": target},
+            device_id_type=MESH,
+        )
+        copy.start()
+        return copy
+
+    right, left, across = at(0, 1), at(0, 3), at(1, 0)
+    mine = at(0, 0)
+    own_right = [send(0, mine, 0, right), None]
+    own_left = [None, send(1, mine, 1, left)]
+    own_across = [send(2, mine, 0, across), None]
+    own_right[1] = send(3, mine, 1, right)
+    own_left[0] = send(4, mine, 0, left)
+    own_across[1] = send(5, mine, 1, across)
+
+    def weigh(shard, part, place, fresh):
+        lines = 16
+
+        def body(step, _):
+            at_row = pl.multiple_of(step * lines, lines)
+            value = gathered[shard, part, pl.ds(at_row, lines), :].astype(jnp.float32)
+            scaled = value * noise_ref[...]
+            weighted[pl.ds(pl.multiple_of(place * rows + at_row, lines), lines), :] = scaled.astype(
+                jnp.bfloat16
+            )
+            total = jnp.sum(scaled * value, axis=1, keepdims=True)
+            here = pl.ds(pl.multiple_of(place * rows + at_row, lines), lines)
+            if fresh:
+                energy[here, :] = jnp.broadcast_to(total, (lines, 128))
+            else:
+                energy[here, :] = energy[here, :] + total
+            return 0
+
+        lax.fori_loop(0, rows // lines, body, 0)
+
+    def multiply(first, second, part, fresh):
+        weigh(first, part, 0, fresh)
+        weigh(second, part, 1, fresh)
+        width = 256
+
+        def body(step, _):
+            column = pl.ds(pl.multiple_of(step * width, width), width)
+            product = lax.dot_general(
+                weighted[...], images[part, column, :], contract_last,
+                preferred_element_type=jnp.float32,
+            )
+            if not fresh:
+                product = product - 0.5 * jnp.tile(energy[...], (1, width // 128))
+            for place, shard in enumerate((first, second)):
+                block = product[place * rows : (place + 1) * rows]
+                there = pl.ds(pl.multiple_of(shard * rows, 16), rows)
+                if fresh:
+                    out_ref[there, column] = block
+                else:
+                    out_ref[there, column] = out_ref[there, column] + block
+            return 0
+
+        lax.fori_loop(0, images.shape[1] // width, body, 0)
+
+    own_right[0].wait_recv()
+    next_right = send(6, at(0, 3), 0, right)
+    own_left[1].wait_recv()
+    next_left = send(7, at(0, 1), 1, left)
+    load.wait()
+    own_across[0].wait_recv()
+    over_right = [send(8, at(1, 0), 0, right), None]
+    over_left = [send(9, at(1, 0), 0, left), None]
+    multiply(at(0, 0), at(1, 0), 0, True)
+    own_across[1].wait_recv()
+    over_right[1] = send(10, at(1, 0), 1, right)
+    over_left[1] = send(11, at(1, 0), 1, left)
+    multiply(at(0, 0), at(1, 0), 1, False)
+    own_right[1].wait_recv()
+    own_left[0].wait_recv()
+    next_right.wait_recv()
+    over_across = [send(12, at(0, 2), 0, across), None]
+    next_left.wait_recv()
+    over_across[1] = send(13, at(0, 2), 1, across)
+    multiply(at(0, 1), at(0, 3), 0, True)
+    multiply(at(0, 1), at(0, 3), 1, False)
+    over_right[0].wait_recv()
+    over_left[0].wait_recv()
+    multiply(at(1, 1), at(1, 3), 0, True)
+    over_right[1].wait_recv()
+    over_left[1].wait_recv()
+    multiply(at(1, 1), at(1, 3), 1, False)
+    over_across[0].wait_recv()
+    multiply(at(0, 2), at(1, 2), 0, True)
+    over_across[1].wait_recv()
+    multiply(at(0, 2), at(1, 2), 1, False)
+    for copy in (
+        own_right + own_left + own_across + [next_right, next_left]
+        + over_right + over_left + over_across
+    ):
+        copy.wait_send()
+
+
+def gathered_scores(references, noise_weight, images, image_groups):
+    parts, rows, freqs = references.shape
+    count = images.shape[1]
+    return pl.pallas_call(
+        score_kernel,
+        out_shape=jax.ShapeDtypeStruct((image_groups * rows, count), jnp.float32),
+        in_specs=[pl.BlockSpec(memory_space=VMEM)] * 2 + [pl.BlockSpec(memory_space=pl.ANY)],
+        out_specs=pl.BlockSpec(memory_space=VMEM),
+        scratch_shapes=[
+            VMEM(images.shape, jnp.bfloat16),
+            VMEM((image_groups, parts, rows, freqs), jnp.bfloat16),
+            VMEM((2 * rows, freqs), jnp.bfloat16),
+            VMEM((2 * rows, 128), jnp.float32),
+            DMA(()),
+            DMA(()),
+            DMA((14,)),
+            DMA((14,)),
+        ],
+        compiler_params=pltpu.CompilerParams(
+            collective_id=0, has_side_effects=True, vmem_limit_bytes=VMEM_BYTES
+        ),
+    )(references, noise_weight.reshape(1, freqs), images)
+
+
+def posterior_kernel(
+    windows_ref, fine_ref, out_ref, pair_in, chip_out, chip_in,
+    pair_send, pair_recv, chip_send, chip_recv, gat_send, gat_recv, sib_send, sib_recv,
+):
+    me = lax.axis_index("freq")
+    core = me % 2
+    z, y = me // 8, me // 2 % 4
+    count = windows_ref.shape[0] // 16
+    sibling = me + 1 - 2 * core
+    spots = [(dz, dy) for dz, dy in ((1, 2), (1, 1), (1, 3), (0, 2), (1, 0), (0, 1), (0, 3), (0, 0))]
+    target = lambda dz, dy: (z + dz) % 2 * 8 + (y + dy) % 4 * 2 + core
+    source = lambda dz, dy: (z + dz) % 2 * 8 + (y + 4 - dy) % 4 * 2 + core
+    greet("freq", [target(*spot) for spot in spots[:-1]] + [sibling])
+    lines = lambda block: pl.ds(pl.multiple_of(block * count, 16), count)
+
+    def send(src, dst, send_sem, recv_sem, other):
+        copy = pltpu.make_async_remote_copy(
+            src_ref=src, dst_ref=dst, send_sem=send_sem, recv_sem=recv_sem,
+            device_id={"freq": other}, device_id_type=MESH,
+        )
+        copy.start()
+        return copy
+
+    pairs = []
+    for n, spot in enumerate(spots):
+        block = target(*spot) + 1 - 2 * core
+        pairs.append(
+            send(windows_ref.at[lines(block)], pair_in.at[n], pair_send.at[n], pair_recv.at[n], sibling)
+        )
+    chips = []
+    for n, spot in enumerate(spots):
+        pairs[n].wait_recv()
+        total = windows_ref[lines(target(*spot)), :] + pair_in[n]
+        if n == 7:
+            break
+        chip_out[n] = total
+        chips.append(
+            send(chip_out.at[n], chip_in.at[n], chip_send.at[n], chip_recv.at[n], target(*spot))
+        )
+    chip_out[7] = total
+    scores = chip_out[7]
+    for n in range(7):
+        chips[6 - n].wait_recv()
+        scores = scores + chip_in[6 - n]
+    fine = fine_ref[...]
+    position = lax.broadcasted_iota(jnp.int32, scores.shape, 1)
+    inside = (position >= fine) & (position <= fine + 224)
     logits = jnp.where(inside, tempering * scores, masked_logit)
     raised = jnp.where(inside, jnp.exp(logits - jnp.max(logits, axis=1, keepdims=True)), 0.0)
-    return raised / jnp.sum(raised, axis=1, keepdims=True)
+    result = raised / jnp.sum(raised, axis=1, keepdims=True)
+    out_ref[lines(me), :] = result.astype(jnp.bfloat16)
+    gathers, relays = [], []
+    for n, spot in enumerate(spots[:-1]):
+        here = out_ref.at[lines(me)]
+        gathers.append(send(here, here, gat_send.at[n], gat_recv.at[n], target(*spot)))
+    here = out_ref.at[lines(me)]
+    relays.append(send(here, here, sib_send.at[7], sib_recv.at[7], sibling))
+    for n in range(6, -1, -1):
+        gathers[n].wait_recv()
+        here = out_ref.at[lines(source(*spots[n]))]
+        relays.append(send(here, here, sib_send.at[n], sib_recv.at[n], sibling))
+    for copy in relays:
+        copy.wait_recv()
+    for copy in pairs + chips + gathers + relays:
+        copy.wait_send()
+
+
+def windowed_posterior(windows, own_fine):
+    rows, width = windows.shape
+    count = rows // 16
+    sems = [DMA((8,)) for _ in range(8)]
+    return pl.pallas_call(
+        posterior_kernel,
+        out_shape=jax.ShapeDtypeStruct((rows, width), jnp.bfloat16),
+        in_specs=[pl.BlockSpec(memory_space=VMEM)] * 2,
+        out_specs=pl.BlockSpec(memory_space=VMEM),
+        scratch_shapes=[VMEM((8, count, width), jnp.float32) for _ in range(3)] + sems,
+        compiler_params=pltpu.CompilerParams(
+            collective_id=1, has_side_effects=True, vmem_limit_bytes=VMEM_BYTES
+        ),
+    )(windows, own_fine)
+
+
+def sums_kernel(
+    rounded_ref, images_hbm, out_ref, images, lhs, part, first_in, side_in, half_in, near_in,
+    last_in, load_sem, send_sem, recv_sem,
+):
+    at = img_neighbours()
+    rows, freqs = out_ref.shape[1:]
+    loads = []
+    for n in range(2):
+        loads.append(pltpu.make_async_copy(images_hbm.at[n], images.at[n], load_sem.at[n]))
+        loads[-1].start()
+    right, left, across = at(0, 1), at(0, 3), at(1, 0)
+    greet("img", [right, left, across])
+
+    def multiply(first, second, n):
+        for place, (other, shift) in enumerate((first, second)):
+            there = pl.ds(pl.multiple_of(at(other, shift) * rows, 16), rows)
+            lhs[place * rows : (place + 1) * rows, :] = rounded_ref[there, :]
+        width = 256
+
+        def body(step, _):
+            column = pl.ds(pl.multiple_of(step * width, width), width)
+            product = jnp.dot(
+                lhs[...], images[n, :, column], preferred_element_type=jnp.float32
+            ).astype(jnp.bfloat16)
+            for place, (other, shift) in enumerate((first, second)):
+                part[other * 4 + shift, n, :, column] = product[place * rows : (place + 1) * rows]
+            return 0
+
+        lax.fori_loop(0, freqs // width, body, 0)
+
+    copies = []
+
+    def send(src, dst, target):
+        number = len(copies)
+        copy = pltpu.make_async_remote_copy(
+            src_ref=src, dst_ref=dst, send_sem=send_sem.at[number], recv_sem=recv_sem.at[number],
+            device_id={"img": target}, device_id_type=MESH,
+        )
+        copy.start()
+        copies.append(copy)
+        return copy
+
+    def combine(dst, sources):
+        lines = 16
+
+        def body(step, _):
+            here = pl.ds(pl.multiple_of(step * lines, lines), lines)
+            total = sources[0][here, :].astype(jnp.float32)
+            for source in sources[1:]:
+                total = total + source[here, :].astype(jnp.float32)
+            dst[here, :] = total.astype(dst.dtype)
+            return 0
+
+        lax.fori_loop(0, rows // lines, body, 0)
+
+    first, sides, near = [], [[], []], [[None, None], [None, None]]
+    for n in range(2):
+        loads[n].wait()
+        multiply((1, 2), (0, 2), n)
+        first.append(send(part.at[6, n], first_in.at[n], across))
+    for n in range(2):
+        multiply((1, 1), (1, 3), n)
+        sides[0].append(send(part.at[5, n], side_in.at[0, n], right))
+        sides[1].append(send(part.at[7, n], side_in.at[1, n], left))
+    for n in range(2):
+        multiply((0, 1), (0, 3), n)
+    halves = []
+    first[0].wait_recv()
+    combine(part.at[2, 0], [part.at[2, 0], first_in.at[0]])
+    halves.append(send(part.at[2, 0], half_in.at[0], left))
+    for n in range(2):
+        multiply((1, 0), (0, 0), n)
+    first[1].wait_recv()
+    combine(part.at[2, 1], [part.at[2, 1], first_in.at[1]])
+    halves.append(send(part.at[2, 1], half_in.at[1], right))
+    near[0][0] = send(part.at[1, 0], near_in.at[0, 0], right)
+    near[1][1] = send(part.at[3, 1], near_in.at[1, 1], left)
+    last = []
+    for n in range(2):
+        sides[0][n].wait_recv()
+        sides[1][n].wait_recv()
+        combine(part.at[4, n], [part.at[4, n], side_in.at[0, n], side_in.at[1, n]])
+        last.append(send(part.at[4, n], last_in.at[n], across))
+    halves[0].wait_recv()
+    combine(part.at[3, 0], [part.at[3, 0], half_in.at[0]])
+    near[1][0] = send(part.at[3, 0], near_in.at[1, 0], left)
+    halves[1].wait_recv()
+    combine(part.at[1, 1], [part.at[1, 1], half_in.at[1]])
+    near[0][1] = send(part.at[1, 1], near_in.at[0, 1], right)
+    for n in range(2):
+        near[0][n].wait_recv()
+        near[1][n].wait_recv()
+        last[n].wait_recv()
+        combine(
+            out_ref.at[n], [part.at[0, n], near_in.at[0, n], near_in.at[1, n], last_in.at[n]]
+        )
+    for copy in copies:
+        copy.wait_send()
+
+
+def scattered_sums(rounded, images, image_groups):
+    rows = rounded.shape[0] // image_groups
+    parts, count, freqs = images.shape
+    block = (parts, rows, freqs)
+    return pl.pallas_call(
+        sums_kernel,
+        out_shape=jax.ShapeDtypeStruct(block, jnp.float32),
+        in_specs=[pl.BlockSpec(memory_space=VMEM), pl.BlockSpec(memory_space=pl.ANY)],
+        out_specs=pl.BlockSpec(memory_space=VMEM),
+        scratch_shapes=[
+            VMEM(images.shape, jnp.bfloat16),
+            VMEM((2 * rows, count), jnp.bfloat16),
+            VMEM((image_groups, *block), jnp.bfloat16),
+            VMEM(block, jnp.bfloat16),
+            VMEM((2, *block), jnp.bfloat16),
+            VMEM(block, jnp.bfloat16),
+            VMEM((2, *block), jnp.bfloat16),
+            VMEM(block, jnp.bfloat16),
+            DMA((2,)),
+            DMA((14,)),
+            DMA((14,)),
+        ],
+        compiler_params=pltpu.CompilerParams(
+            collective_id=2, has_side_effects=True, vmem_limit_bytes=VMEM_BYTES
+        ),
+    )(rounded, images)
 
 
 def spread_taps(values, kernels, kernel_taps):
@@ -100,37 +464,18 @@
     orient_count = local_orients * image_groups
     share_rows = orient_count // freq_groups
     share_images = images.shape[1] // freq_groups
-    unpacked = lax.all_gather(references, "img", axis=1, tiled=True).astype(jnp.float32)
-    weighted = (noise_weight * unpacked).astype(jnp.bfloat16)
-    energies = jnp.sum(
-        noise_weight * (unpacked[0] * unpacked[0] + unpacked[1] * unpacked[1]), axis=1
-    )
-    products = lax.dot_general(
-        weighted[0], images[0], contract_last, preferred_element_type=jnp.float32
-    )
-    products = products + lax.dot_general(
-        weighted[1], images[1], contract_last, preferred_element_type=jnp.float32
-    )
-    partial_scores = products - 0.5 * energies[:, None]
+    partial_scores = gathered_scores(references, noise_weight, images, image_groups)
     windows = to_windows(partial_scores, prior_orient).T
-    scores = lax.psum_scatter(windows, "freq", scatter_dimension=0, tiled=True)
     own_prior = lax.dynamic_slice_in_dim(
         prior_orient, lax.axis_index("freq") * share_images, share_images, 0
     )
-    kept = window_softmax(scores, own_prior, orient_count).astype(jnp.bfloat16)
-    kept = lax.all_gather(kept, "freq", axis=0, tiled=True).T
+    own_fine = window_parts(own_prior, orient_count)[1] % FINE[-1]
+    kept = windowed_posterior(windows, own_fine[:, None]).T
     rounded = from_windows(kept, prior_orient, orient_count)
     own_rows = lax.dynamic_slice_in_dim(
         rounded, lax.axis_index("freq") * share_rows, share_rows, 0
     ).astype(jnp.float32)
-    weighted_sums = lax.psum_scatter(
-        jnp.einsum("oi,cif->cof", rounded, images, preferred_element_type=jnp.float32).astype(
-            jnp.bfloat16
-        ),
-        "img",
-        scatter_dimension=1,
-        tiled=True,
-    ).astype(jnp.float32)
+    weighted_sums = scattered_sums(rounded, images, image_groups)
     segment_blocks = segment_row.shape[2]
     lane_count = images.shape[2] // segment_blocks
     local_segments = local_orients * segment_blocks

time: 463 us -> 319 us (0.69)
  waiting for transfers between devices: 255 us -> 34.8 us
  Pallas kernels: 0 us -> 168 us
  matrix products: 56.6 us -> 25.9 us
  other arithmetic: 53.7 us -> 26.8 us
  blocking collectives: 26.3 us -> 0 us
  between operations: 14.5 us -> 1.17 us
  local copies, waits for them, and re-layouts: 34.4 us -> 39.4 us
  starting transfers between devices: 13.1 us -> 18 us
    pallas_call x0 -> x3, Pallas kernels: none -> 168 us  [the longest x1 71.5 us: gathered_scores(): pl.pallas_call(score_kernel, out_shape=jax.ShapeDtypeStruct((image_groups...]
    reduce_scatter x2 -> x0, waiting for transfers between devices: 134 us -> none  [the longest x1 68.7 us: on_device(): lax.psum_scatter(jnp.einsum('oi,cif->cof', rounded, images, preferred_ele...]
    all_gather x1 -> x0, waiting for transfers between devices: 86.2 us -> none  [on_device(): lax.all_gather(references, 'img', axis=1, tiled=True).astype(jnp.float32)]
    dot_general x3 -> x0, matrix products: 30.7 us -> none  [the longest x1 13.3 us: on_device(): jnp.einsum('oi,cif->cof', rounded, images, preferred_element_type=jnp.flo...]
    all_gather x1 -> x0, blocking collectives: 26.3 us -> none  [on_device(): kept = lax.all_gather(kept, 'freq', axis=0, tiled=True).T]
    convert_element_type x3 -> x0, other arithmetic: 16.8 us -> none  [the longest x1 10.1 us: on_device(): lax.all_gather(references, 'img', axis=1, tiled=True).astype(jnp.float32)]
    convert_element_type x1, other arithmetic: 12.8 us -> 2.8 us  [on_device(): spread_taps(values, kernels, kernel_taps).astype(jnp.bfloat16)]
    pallas_call x0 -> x2, local copies, waits for them, and re-layouts: none -> 7.52 us  [the longest x1 6.11 us: gathered_scores(): pl.pallas_call(score_kernel, out_shape=jax.ShapeDtypeStruct((image_groups...]
  transfers between devices with their start and end apart: 5 -> 2, of which waited for: 4 -> 1; matrix products, arithmetic and copies ran while one was open for 13% -> 21% of each run, Pallas kernels for 0% -> 54%
where the time goes in v2:
time: 319 us; the launch traced here: 314 us
  Pallas kernels  168 us (53%)
  local copies, waits for them, and re-layouts  39.4 us (12%)
  waiting for transfers between devices  34.8 us (11%)
  other arithmetic  26.8 us (8%)
  matrix products  25.9 us (8%)
  starting transfers between devices  18 us (6%)
    pallas_call x1, Pallas kernels, gathered_scores(): pl.pallas_call(score_kernel, out_shape=jax.ShapeDtypeStruct((image_groups...  71.5 us
    pallas_call x1, Pallas kernels, scattered_sums(): pl.pallas_call(sums_kernel, out_shape=jax.ShapeDtypeStruct(block, jnp.flo...  66.8 us
    all_to_all x2, waiting for transfers between devices, on_device(): lax.all_to_all(lines.reshape(brick_count, capacity, -1), ('img', 'freq'),...  34.8 us
    pallas_call x1, Pallas kernels, windowed_posterior(): pl.pallas_call(posterior_kernel, out_shape=jax.ShapeDtypeStruct((rows, wi...  30 us
    another operation x1, local copies, waits for them, and re-layouts, on_device(): jnp.stack([jnp.dot(hits, part, preferred_element_type=jnp.float32) for pa...  19.5 us
    all_to_all x2, starting transfers between devices, on_device(): lax.all_to_all(lines.reshape(brick_count, capacity, -1), ('img', 'freq'),...  18 us
    dot_general x2, matrix products, on_device(): jnp.dot(row_member.astype(jnp.bfloat16), arrived[:, part * lane_count:(pa...  13.9 us
    dot_general x2, matrix products, on_device(): jnp.dot(hits, part, preferred_element_type=jnp.float32)  11.3 us
  transfers between devices with their start and end apart: 2, of which 1 were waited for; matrix products, arithmetic and copies ran while one was open for 21% of the time, Pallas kernels for 54%

profile of v2, /device:TPU:1, one launch (start us, length us, event | category | flops | bytes accessed | tf_op | source)
XLA Modules:
  0.0 314.3 jit_solution(2972226621708168018)
XLA Ops:
  0.6 0.0 copy-start
  0.6 0.8 reshape.64
  1.4 1.2 convert_reduce_fusion
  2.6 0.8 broadcast_in_dim.264
  3.4 3.3 %select_reduce_fusion = s32[4480]{0:T(1024)S(1)} fusion(s32[1792]{0:T(1024)S(1)} %broadcast_in_dim.264, s32[1792]{0:T(1024)S(1)} %multiply_add_fusion), kind=kLoop, calls=%fused_computation.3 | loop fusion | flops 24080000 | bytes 32256 | tf_op jit(solution)/shard_map/reduce_sum | solution.py:498
  6.7 0.8 reshape.66
  7.5 12.1 %all-to-all-start = ((s32[128,35,1]{1,2,0:T(1,128)}), s32[128,35,1]{1,2,0:T(1,128)S(1)}, u32[]{:S(2)}, u32[]{:S(2)}) async-start(s32[128,35,1]{1,2,0:T(1,128)} %bitcast.8), calls=%async_computation | async-start | bytes 131072 | tf_op jit(solution)/shard_map/all_to_all | solution.py:504
  19.6 0.7 fusion.43
  20.3 71.5 %shard_map.95 = f32[896,1536]{1,0:T(8,128)} custom-call(bf16[2,112,2048]{2,1,0:T(8,128)(2,1)} %refs_ref.1, f32[1,2048]{1,0:T(1,128)} %bitcast.44, bf16[2,1536,2048]{2,1,0:T(8,128)(2,1)} %images_hbm.3), custom_call_target="tpu_custom_call" | custom-call | tf_op jit(solution)/shard_map/pallas_call | solution.py:201
  91.8 6.1 %copy.43 = f32[896,1536]{0,1:T(8,128)} copy(f32[896,1536]{1,0:T(8,128)} %shard_map.95) | data formatting | bytes 11010048 | tf_op jit(solution)/shard_map/pallas_call | solution.py:201
  98.0 0.0 slice-start
  98.0 0.9 fusion.50
  98.9 0.7 copy.49.fine_ref
  99.6 0.0 slice-done
  99.6 7.2 %fusion.19 = f32[376,1536]{0,1:T(8,128)S(1)} fusion(f32[896,1536]{0,1:T(8,128)} %copy.43, f32[248,1536]{0,1:T(8,128)S(1)} %slice-done, pred[1536]{0:T(1024)(128)(4,1)S(1)} %get-tuple-element.25, pred[1536]{0:T(1024)(128)(4,1)S(1)} %get-tuple-element.24, pred[1536]{0:T(1024)(128)(4,1)S(1)} %get-tuple-element.26, pred[1536]{0:T(1024)(128)(4,1)S(1)} %get-tuple-element.13, ...), kind=kLoop, calls=%fused_computation.31 | loop fusion | flops 4620288 | bytes 21144576 | tf_op jit(solution)/shard_map/jit(_where)/select_n | solution.py:37
  106.8 0.9 slice_select_fusion.2
  107.8 0.9 slice_select_fusion.1
  108.7 0.9 slice_select_fusion
  109.7 1.8 fusion.27.windows_ref
  111.5 30.0 %shard_map.96 = bf16[1536,256]{1,0:T(8,128)(2,1)} custom-call(f32[1536,256]{1,0:T(8,128)} %fusion.27.windows_ref, s32[96,1]{1,0:T(8,128)} %copy.49.fine_ref), custom_call_target="tpu_custom_call" | custom-call | tf_op jit(solution)/shard_map/pallas_call | solution.py:293
  141.5 1.4 copy.50
  142.9 0.1 pad_select_fusion.3
  143.0 0.1 pad_select_fusion.2
  143.2 0.2 pad_select_fusion.1
  143.3 0.2 pad_select_fusion
  143.5 0.2 select_dynamic-update-slice_fusion.6
  143.7 0.2 select_dynamic-update-slice_fusion.5
  143.9 0.2 select_dynamic-update-slice_fusion.4
  144.1 0.2 select_dynamic-update-slice_fusion.3
  144.3 0.2 select_dynamic-update-slice_fusion.2
  144.5 0.2 select_dynamic-update-slice_fusion.1
  144.7 0.2 select_dynamic-update-slice_fusion.rounded_ref
  144.8 0.0 copy-start.2
  144.9 1.5 copy-done.2
  146.4 66.8 %shard_map.97 = f32[2,112,2048]{2,1,0:T(8,128)} custom-call(bf16[896,1536]{1,0:T(8,128)(2,1)} %copy-done.2, bf16[2,1536,2048]{2,1,0:T(8,128)(2,1)} %images_hbm.3), custom_call_target="tpu_custom_call" | custom-call | tf_op jit(solution)/shard_map/pallas_call | solution.py:409
  213.2 0.0 copy-start.4
  213.2 1.6 copy_bitcast_fusion
  214.8 0.0 copy-done.4
  214.8 0.1 eq.151
  214.9 0.0 copy-done
  214.9 0.6 fusion.30
  215.6 0.1 slice_reduce_fusion.3
  215.7 2.8 fusion.24
  218.5 5.7 %fusion.11 = bf16[4480,1,128]{2,0,1:T(8,128)(2,1)S(1)} fusion(s32[1792]{0:T(1024)S(1)} %multiply_add_fusion, bf16[2,1792,128]{2,1,0:T(8,128)(2,1)S(1)} %fusion.24), kind=kOutput, calls=%fused_computation.16 | convolution fusion | flops 2063810560 | bytes 1613824 | tf_op jit(solution)/shard_map/dot_general | solution.py:502
  224.1 5.7 %fusion.12 = bf16[4480,1,128]{2,0,1:T(8,128)(2,1)S(1)} fusion(s32[1792]{0:T(1024)S(1)} %multiply_add_fusion, bf16[2,1792,128]{2,1,0:T(8,128)(2,1)S(1)} %fusion.24), kind=kOutput, calls=%fused_computation.17 | convolution fusion | flops 2063810560 | bytes 1613824 | tf_op jit(solution)/shard_map/dot_general | solution.py:502
  229.8 0.2 pad_maximum_fusion.1
  230.0 19.5 %copy.53 = bf16[4480,2,128]{2,1,0:T(2,128)(2,1)S(1)} copy(bf16[4480,2,128]{2,0,1:T(8,128)(2,1)S(1)} %pad_maximum_fusion.1) | data formatting | bytes 4587520 | tf_op jit(solution)/shard_map/stack | solution.py:501
  249.5 2.8 convert_element_type.25
  252.3 0.0 all-to-all-done
  252.3 5.9 %all-to-all-start.1 = ((bf16[128,35,256]{2,1,0:T(8,128)(2,1)}), bf16[128,35,256]{2,1,0:T(8,128)(2,1)S(1)}, u32[]{:S(2)}, u32[]{:S(2)}) async-start(bf16[128,35,256]{2,1,0:T(8,128)(2,1)} %convert_element_type.25), calls=%async_computation.1 | async-start | bytes 5242880 | tf_op jit(solution)/shard_map/all_to_all | solution.py:504
  258.2 1.7 dynamic-slice_convert_fusion
  259.9 0.5 broadcast.141
  260.4 0.8 reduce.11
  261.2 0.2 eq.147
  261.4 34.8 %all-to-all-done.1 = bf16[128,35,256]{2,1,0:T(8,128)(2,1)S(1)} async-done(((bf16[128,35,256]{2,1,0:T(8,128)(2,1)}), bf16[128,35,256]{2,1,0:T(8,128)(2,1)S(1)}, u32[]{:S(2)}, u32[]{:S(2)}) %all-to-all-start.1) | async-done | bytes 2293792 | tf_op jit(solution)/shard_map/all_to_all | solution.py:504
  296.2 2.4 reshape.70
  298.6 0.0 copy-start.3
  298.6 7.7 %fusion.13 = f32[1,2000,128]{2,1,0:T(8,128)S(1)} fusion(s32[4480]{0:T(1024)S(1)} %eq.147, bf16[4480,256]{1,0:T(8,128)(2,1)} %reshape.70), kind=kOutput, calls=%fused_computation.21 | convolution fusion | flops 2302720000 | bytes 2188800 | tf_op jit(solution)/shard_map/dot_general | solution.py:516
  306.3 0.0 copy-done.3
  306.4 0.0 copy-start.1
  306.4 6.2 %fusion.14 = f32[1,2000,128]{2,1,0:T(8,128)S(1)} fusion(s32[4480]{0:T(1024)S(1)} %eq.147, bf16[4480,256]{1,0:T(8,128)(2,1)S(1)} %copy-done.3), kind=kOutput, calls=%fused_computation.22 | convolution fusion | flops 2302720000 | bytes 2191360 | tf_op jit(solution)/shard_map/dot_general | solution.py:516
  312.6 1.4 maximum_bitcast_fusion
  314.0 0.0 copy-done.1
  (2 shorter events, 0.0 us)
Async XLA Ops:
  0.6 214.3 %copy-start = (f32[8,4]{0,1:T(4,128)S(1)}, f32[8,4]{0,1:T(4,128)}, u32[]{:S(2)}) copy-start(f32[8,4]{0,1:T(4,128)} %param.15) | copy-start | bytes 388
  7.5 244.8 %all-to-all-start = ((s32[128,35,1]{1,2,0:T(1,128)}), s32[128,35,1]{1,2,0:T(1,128)S(1)}, u32[]{:S(2)}, u32[]{:S(2)}) async-start(s32[128,35,1]{1,2,0:T(1,128)} %bitcast.8), calls=%async_computation | async-start | bytes 131072 | tf_op jit(solution)/shard_map/all_to_all | solution.py:504
  98.0 1.7 slice-start
  144.8 1.6 copy-start.2
  213.2 1.6 copy-start.4
  252.3 43.9 %all-to-all-start.1 = ((bf16[128,35,256]{2,1,0:T(8,128)(2,1)}), bf16[128,35,256]{2,1,0:T(8,128)(2,1)S(1)}, u32[]{:S(2)}, u32[]{:S(2)}) async-start(bf16[128,35,256]{2,1,0:T(8,128)(2,1)} %convert_element_type.25), calls=%async_computation.1 | async-start | bytes 5242880 | tf_op jit(solution)/shard_map/all_to_all | solution.py:504
  298.6 7.7 %copy-start.3 = (bf16[4480,256]{1,0:T(8,128)(2,1)S(1)}, bf16[4480,256]{1,0:T(8,128)(2,1)}, u32[]{:S(2)}) copy-start(bf16[4480,256]{1,0:T(8,128)(2,1)} %reshape.70) | copy-start | bytes 6881284
  306.4 7.7 %copy-start.1 = (f32[8,4]{0,1:T(4,128)S(1)}, f32[8,4]{0,1:T(4,128)}, u32[]{:S(2)}) copy-start(f32[8,4]{0,1:T(4,128)} %param.15) | copy-start | bytes 388

commit v3 on v2

--- a/solution.py
+++ b/solution.py
@@ -430,22 +430,210 @@
     )(rounded, images)
 
 
-def spread_taps(values, kernels, kernel_taps):
-    phases, tap_count = kernel_taps.shape
-    member = (kernels[:, None] == jnp.arange(phases, dtype=jnp.int32)[None, :]).astype(
-        kernel_taps.dtype
+def exchange_kernel(
+    sums_ref, factor_ref, place_ref, table_ref, out_ref, values, packed, arrived, lines_in,
+    members, terms, total, send_sem, recv_sem, line_send, line_recv, own_sem,
+):
+    groups, wide = 8, 16
+    img, freq = lax.axis_index("img"), lax.axis_index("freq")
+    slots = packed.shape[1] // 2
+    segments = values.shape[0]
+    rows, lanes = sums_ref.shape[1], sums_ref.shape[2] // (segments // sums_ref.shape[1])
+    barrier = pltpu.get_barrier_semaphore()
+
+    def everyone(visit):
+        def outer(di, _):
+            def inner(df, _):
+                @pl.when((di > 0) | (df > 0))
+                def _():
+                    visit(di, (img + di) % groups, (freq + df) % wide)
+
+                return 0
+
+            return lax.fori_loop(0, wide, inner, 0)
+
+        lax.fori_loop(0, groups, outer, 0)
+
+    everyone(
+        lambda di, to_img, to_freq: pl.semaphore_signal(
+            barrier, inc=1, device_id={"img": to_img, "freq": to_freq}, device_id_type=MESH
+        )
     )
-    factors = jnp.dot(member, kernel_taps, precision=lax.Precision.HIGHEST)
-    padded = jnp.pad(values, ((0, 0), (0, 0), (tap_count - 2, 1)))
-    lane_count = values.shape[2]
-    result = jnp.zeros(values.shape, values.dtype)
-    for tap_index in range(tap_count):
-        first_lane = tap_count - 1 - tap_index
-        result = (
-            result
-            + factors[None, :, tap_index, None] * padded[:, :, first_lane : first_lane + lane_count]
-        )
-    return result
+    lane = lax.broadcasted_iota(jnp.int32, (rows, lanes), 1)
+    for q in range(segments // rows):
+        for part in range(2):
+            value = sums_ref[part, :, q * lanes : (q + 1) * lanes]
+            shifted = [
+                jnp.where(lane < lanes - 1, pltpu.roll(value, lanes - 1, 1), 0.0),
+                value,
+                jnp.where(lane >= 1, pltpu.roll(value, 1, 1), 0.0),
+                jnp.where(lane >= 2, pltpu.roll(value, 2, 1), 0.0),
+            ]
+            result = factor_ref[q, :, 0:1] * shifted[0]
+            for tap in range(1, 4):
+                result = result + factor_ref[q, :, tap : tap + 1] * shifted[tap]
+            values[q * rows : (q + 1) * rows, part * lanes : (part + 1) * lanes] = result.astype(
+                jnp.bfloat16
+            )
+    me = img * wide + freq
+    pl.semaphore_wait(barrier, groups * wide - 1)
+
+    def send_line(di, to_img, to_freq):
+        pltpu.make_async_remote_copy(
+            src_ref=table_ref.at[to_img * wide + to_freq],
+            dst_ref=lines_in.at[me],
+            send_sem=line_send,
+            recv_sem=line_recv,
+            device_id={"img": to_img, "freq": to_freq},
+            device_id_type=MESH,
+        ).start()
+
+    everyone(send_line)
+    lines_in[me] = table_ref[me]
+
+    def send_group(di, _):
+        to_img = (img + di) % groups
+        some = wide // 2
+
+        def pack(half, _):
+            base = (to_img * wide + half * some) * slots
+            slot = base + lax.broadcasted_iota(jnp.int32, (some * slots, 1), 0)
+            found = jnp.zeros((some * slots, 2 * lanes), jnp.float32)
+            step = 256
+            for first in range(0, segments, step):
+                hit = jnp.where(place_ref[:, first : first + step] == slot, 1.0, 0.0)
+                found = found + jnp.dot(
+                    hit.astype(jnp.bfloat16), values[first : first + step, :],
+                    preferred_element_type=jnp.float32,
+                )
+            for brick in range(some):
+                block = found[brick * slots : (brick + 1) * slots]
+                packed[to_img * wide + half * some + brick] = jnp.concatenate(
+                    [block[:, :lanes], block[:, lanes:]], axis=0
+                ).astype(jnp.bfloat16)
+            return 0
+
+        lax.fori_loop(0, 2, pack, 0)
+
+        def inner(df, _):
+            to_freq = (freq + df) % wide
+
+            @pl.when((di > 0) | (df > 0))
+            def _():
+                pltpu.make_async_remote_copy(
+                    src_ref=packed.at[to_img * wide + to_freq],
+                    dst_ref=arrived.at[me],
+                    send_sem=send_sem,
+                    recv_sem=recv_sem.at[di],
+                    device_id={"img": to_img, "freq": to_freq},
+                    device_id_type=MESH,
+                ).start()
+
+            return 0
+
+        return lax.fori_loop(0, wide, inner, 0)
+
+    lax.fori_loop(0, groups, send_group, 0)
+    own = pltpu.make_async_copy(packed.at[me], arrived.at[me], own_sem)
+    own.start()
+    most = pl.ds(0, groups * wide - 1)
+    pltpu.make_async_copy(lines_in.at[most], lines_in.at[most], line_recv).wait()
+    pltpu.make_async_copy(table_ref.at[most], table_ref.at[most], line_send).wait()
+    place = lax.broadcasted_iota(jnp.int32, (1, 128), 1)
+    chunks = wide * slots // 128
+    row_step = 400
+
+    def make_members(group, _):
+        row_lines = [jnp.zeros((1, 128), jnp.int32) for _ in range(chunks)]
+        for member in range(wide):
+            line = lines_in[group * wide + member]
+            chunk, first = member * slots // 128, member * slots % 128
+            turned = pltpu.roll(line, first, 1) if first else line
+            row_lines[chunk] = jnp.where(
+                (place >= first) & (place < first + slots), turned, row_lines[chunk]
+            )
+            if first + slots > 128:
+                row_lines[chunk + 1] = jnp.where(
+                    place < first + slots - 128, turned, row_lines[chunk + 1]
+                )
+        row_lines = jnp.concatenate(row_lines, axis=1)
+
+        def fill(step, _):
+            first = pl.multiple_of(step * 16, 16)
+            voxel = first + lax.broadcasted_iota(jnp.int32, (16, 1), 0)
+            members[group, pl.ds(first, 16), :] = jnp.where(row_lines == voxel, 1.0, 0.0).astype(
+                jnp.bfloat16
+            )
+            return 0
+
+        return lax.fori_loop(0, BROWS // 16, fill, 0)
+
+    lax.fori_loop(0, groups, make_members, 0)
+    for di in range(groups):
+        group = (img + groups - di) % groups
+        count = wide - 1 if di == 0 else wide
+        some = pl.ds(0, count)
+        pltpu.make_async_copy(arrived.at[some], arrived.at[some], recv_sem.at[di]).wait()
+        if di == 0:
+            own.wait()
+        for pair in range(wide // 2):
+            blocks = [
+                arrived[group * wide + 2 * pair + n].astype(jnp.float32) for n in range(2)
+            ]
+            for part in range(2):
+                both = [block[part * slots : (part + 1) * slots] for block in blocks]
+                terms[2 * pair * slots : 2 * (pair + 1) * slots, part * lanes : (part + 1) * lanes] = (
+                    jnp.concatenate(both, axis=0).astype(jnp.bfloat16)
+                )
+
+        def add(step, _):
+            here = pl.ds(pl.multiple_of(step * row_step, 16), row_step)
+            found = jnp.dot(members[group, here, :], terms[...], preferred_element_type=jnp.float32)
+            if di > 0:
+                found = found + total[here, :]
+            if di < groups - 1:
+                total[here, :] = found
+            else:
+                out_ref[0, 0, here, :] = found[:, :lanes]
+                out_ref[0, 1, here, :] = found[:, lanes:]
+            return 0
+
+        lax.fori_loop(0, BROWS // row_step, add, 0)
+    pltpu.make_async_copy(packed.at[most], packed.at[most], send_sem).wait()
+
+
+def exchanged_volume(sums, factors, places, table, slots):
+    bricks = table.shape[0]
+    segments = places.shape[1]
+    lanes = 128
+    return pl.pallas_call(
+        exchange_kernel,
+        out_shape=jax.ShapeDtypeStruct((1, 2, BROWS, lanes), jnp.float32),
+        in_specs=[pl.BlockSpec(memory_space=VMEM)] * 4,
+        out_specs=pl.BlockSpec(memory_space=VMEM),
+        scratch_shapes=[
+            VMEM((segments, 2 * lanes), jnp.bfloat16),
+            VMEM((bricks, 2 * slots, lanes), jnp.bfloat16),
+            VMEM((bricks, 2 * slots, lanes), jnp.bfloat16),
+            VMEM((bricks, 1, 128), jnp.int32),
+            VMEM((8, BROWS, 16 * slots), jnp.bfloat16),
+            VMEM((16 * slots, 2 * lanes), jnp.bfloat16),
+            VMEM((BROWS, 2 * lanes), jnp.float32),
+            DMA(()),
+            DMA((8,)),
+            DMA(()),
+            DMA(()),
+            DMA(()),
+        ],
+        compiler_params=pltpu.CompilerParams(
+            collective_id=3, has_side_effects=True, vmem_limit_bytes=VMEM_BYTES
+        ),
+    )(sums, factors, places, table)
+
+
+def tap_factors(kernels, kernel_taps):
+    member = kernels[..., None] == jnp.arange(kernel_taps.shape[0], dtype=jnp.int32)
+    return jnp.sum(jnp.where(member[..., None], kernel_taps, 0.0), axis=-2)
 
 
 def on_device(
@@ -477,51 +665,25 @@
     ).astype(jnp.float32)
     weighted_sums = scattered_sums(rounded, images, image_groups)
     segment_blocks = segment_row.shape[2]
-    lane_count = images.shape[2] // segment_blocks
+    by_block = lambda per_segment: per_segment.reshape(local_orients, segment_blocks).T
     local_segments = local_orients * segment_blocks
-    values = weighted_sums.reshape(2, local_orients, segment_blocks, lane_count)
-    values = values.transpose(0, 2, 1, 3).reshape(2, local_segments, lane_count)
-    targets = segment_brick.reshape(local_orients, segment_blocks).T.reshape(-1)
-    voxel_rows = segment_row.reshape(local_orients, segment_blocks).T.reshape(-1)
-    kernels = segment_kernel.reshape(local_orients, segment_blocks).T.reshape(-1)
+    targets = by_block(segment_brick).reshape(-1)
+    voxel_rows = by_block(segment_row).reshape(-1)
+    factors = tap_factors(by_block(segment_kernel), kernel_taps)
     brick_count = image_groups * freq_groups
     capacity = max(2, 5 * local_segments // (2 * brick_count))
+    slots = -(-capacity // 8) * 8
     segment_ids = jnp.arange(local_segments, dtype=jnp.int32)
     same_brick = (targets[:, None] == targets[None, :]) & (
         segment_ids[None, :] < segment_ids[:, None]
     )
-    rank_within = jnp.sum(same_brick.astype(jnp.int32), axis=1)
-    places = targets * capacity + rank_within
-    slot_total = brick_count * capacity
-    slot_ids = jnp.arange(slot_total, dtype=jnp.int32)
-    slot_hits = places[None, :] == slot_ids[:, None]
-    packed_rows = jnp.sum(jnp.where(slot_hits, voxel_rows[None, :], 0), axis=1)
-    contributions = spread_taps(values, kernels, kernel_taps).astype(jnp.bfloat16)
-    hits = slot_hits.astype(jnp.bfloat16)
-    packed = jnp.stack(
-        [jnp.dot(hits, part, preferred_element_type=jnp.float32) for part in contributions], axis=1
-    ).astype(jnp.bfloat16)
-    exchange = lambda lines: lax.all_to_all(
-        lines.reshape(brick_count, capacity, -1),
-        ("img", "freq"),
-        split_axis=0,
-        concat_axis=0,
-        tiled=True,
-    )
-    arrived_rows = exchange(packed_rows).reshape(-1)
-    arrived = exchange(packed).reshape(slot_total, 2 * lane_count)
-    row_member = arrived_rows[None, :] == jnp.arange(BROWS, dtype=jnp.int32)[:, None]
-    volume = jnp.stack(
-        [
-            jnp.dot(
-                row_member.astype(jnp.bfloat16),
-                arrived[:, part * lane_count : (part + 1) * lane_count],
-                preferred_element_type=jnp.float32,
-            )
-            for part in range(2)
-        ]
-    )
-    return (own_rows, volume[None])
+    places = targets * slots + jnp.sum(same_brick.astype(jnp.int32), axis=1)
+    slot_ids = jnp.arange(brick_count * slots, dtype=jnp.int32)
+    hits = places[None, :] == slot_ids[:, None]
+    table = jnp.sum(jnp.where(hits, voxel_rows[None, :], 0), axis=1).reshape(brick_count, 1, slots)
+    table = jnp.pad(table, ((0, 0), (0, 0), (0, 128 - slots)))
+    volume = exchanged_volume(weighted_sums, factors, places[None, :], table, slots)
+    return (own_rows, volume)
 
 
 def solution(mesh):

time: 319 us -> 262 us (0.82)
  Pallas kernels: 168 us -> 220 us
  waiting for transfers between devices: 34.8 us -> 0 us
  matrix products: 25.9 us -> 0 us
  local copies, waits for them, and re-layouts: 39.4 us -> 16.6 us
  starting transfers between devices: 18 us -> 0 us
  other arithmetic: 26.8 us -> 23.2 us
    pallas_call x0 -> x1, Pallas kernels: none -> 50.6 us  [exchanged_volume(): pl.pallas_call(exchange_kernel, out_shape=jax.ShapeDtypeStruct((1, 2, BRO...]
    all_to_all x2 -> x0, waiting for transfers between devices: 34.8 us -> none  [on_device(): lax.all_to_all(lines.reshape(brick_count, capacity, -1), ('img', 'freq'),...]
    dot_general x5 -> x0, matrix products: 25.9 us -> none  [the longest x2 13.9 us: on_device(): jnp.dot(row_member.astype(jnp.bfloat16), arrived[:, part * lane_count:(pa...]
    another operation x1 -> x0, local copies, waits for them, and re-layouts: 19.5 us -> none  [on_device(): jnp.stack([jnp.dot(hits, part, preferred_element_type=jnp.float32) for pa...]
    all_to_all x2 -> x0, starting transfers between devices: 18 us -> none  [on_device(): lax.all_to_all(lines.reshape(brick_count, capacity, -1), ('img', 'freq'),...]
    reshape x4 -> x1, local copies, waits for them, and re-layouts: 5.65 us -> 0.09 us  [on_device(): jnp.sum(jnp.where(hits, voxel_rows[None, :], 0), axis=1)]
  transfers between devices with their start and end apart: 2 -> 0, of which waited for: 1 -> 0; matrix products, arithmetic and copies ran while one was open for 21% -> 0% of each run, Pallas kernels for 54% -> 0%
where the time goes in v3:
time: 262 us; the launch traced here: 260 us
  Pallas kernels  220 us (84%)
  other arithmetic  23.2 us (9%)
  local copies, waits for them, and re-layouts  16.6 us (6%)
    pallas_call x1, Pallas kernels, gathered_scores(): pl.pallas_call(score_kernel, out_shape=jax.ShapeDtypeStruct((image_groups...  71.8 us
    pallas_call x1, Pallas kernels, scattered_sums(): pl.pallas_call(sums_kernel, out_shape=jax.ShapeDtypeStruct(block, jnp.flo...  66.7 us
    pallas_call x1, Pallas kernels, exchanged_volume(): pl.pallas_call(exchange_kernel, out_shape=jax.ShapeDtypeStruct((1, 2, BRO...  50.6 us
    pallas_call x1, Pallas kernels, windowed_posterior(): pl.pallas_call(posterior_kernel, out_shape=jax.ShapeDtypeStruct((rows, wi...  30.4 us
    select_n x1, other arithmetic, to_windows(): jnp.where((coarse == block)[None], ring[block * COARSE:block * COARSE + r...  7.54 us
    pallas_call x1, local copies, waits for them, and re-layouts, gathered_scores(): pl.pallas_call(score_kernel, out_shape=jax.ShapeDtypeStruct((image_groups...  6.18 us

profile of v3, /device:TPU:1, one launch (start us, length us, event | category | flops | bytes accessed | tf_op | source)
XLA Modules:
  0.0 260.1 jit_solution(6197857639806976177)
XLA Ops:
  0.6 0.7 fusion.18
  1.4 71.8 %shard_map.95 = f32[896,1536]{1,0:T(8,128)} custom-call(bf16[2,112,2048]{2,1,0:T(8,128)(2,1)} %refs_ref.1, f32[1,2048]{1,0:T(1,128)} %bitcast.20, bf16[2,1536,2048]{2,1,0:T(8,128)(2,1)} %images_hbm.3), custom_call_target="tpu_custom_call" | custom-call | tf_op jit(solution)/shard_map/pallas_call | solution.py:201
  73.2 6.2 %copy.32 = f32[896,1536]{0,1:T(8,128)} copy(f32[896,1536]{1,0:T(8,128)} %shard_map.95) | data formatting | bytes 11010048 | tf_op jit(solution)/shard_map/pallas_call | solution.py:201
  79.4 0.0 slice-start
  79.4 1.4 slice-done
  80.8 7.5 %fusion.5 = f32[376,1536]{0,1:T(8,128)S(1)} fusion(f32[896,1536]{0,1:T(8,128)} %copy.32, f32[248,1536]{0,1:T(8,128)S(1)} %slice-done, pred[1536]{0:T(1024)(128)(4,1)S(1)} %get-tuple-element.21, pred[1536]{0:T(1024)(128)(4,1)S(1)} %get-tuple-element.20, pred[1536]{0:T(1024)(128)(4,1)S(1)} %get-tuple-element.22, pred[1536]{0:T(1024)(128)(4,1)S(1)} %get-tuple-element.9, ...), kind=kLoop, calls=%fused_computation.13 | loop fusion | flops 4620288 | bytes 21144576 | tf_op jit(solution)/shard_map/jit(_where)/select_n | solution.py:37
  88.3 1.0 slice_select_fusion.2
  89.3 1.0 slice_select_fusion.1
  90.3 1.0 slice_select_fusion
  91.3 1.8 fusion.6.windows_ref
  93.1 0.8 fusion.25
  93.9 0.7 copy.38.fine_ref
  94.6 30.4 %shard_map.96 = bf16[1536,256]{1,0:T(8,128)(2,1)} custom-call(f32[1536,256]{1,0:T(8,128)} %fusion.6.windows_ref, s32[96,1]{1,0:T(8,128)} %copy.38.fine_ref), custom_call_target="tpu_custom_call" | custom-call | tf_op jit(solution)/shard_map/pallas_call | solution.py:293
  125.1 1.4 copy.39
  126.5 0.1 pad_select_fusion.3
  126.6 0.1 pad_select_fusion.2
  126.8 0.2 pad_select_fusion.1
  127.0 0.2 pad_select_fusion
  127.1 0.2 select_dynamic-update-slice_fusion.6
  127.3 0.2 select_dynamic-update-slice_fusion.5
  127.5 0.2 select_dynamic-update-slice_fusion.4
  127.7 0.2 select_dynamic-update-slice_fusion.3
  127.9 0.2 select_dynamic-update-slice_fusion.2
  128.1 0.2 select_dynamic-update-slice_fusion.1
  128.3 0.2 select_dynamic-update-slice_fusion.rounded_ref
  128.5 0.0 copy-start
  128.5 1.5 copy-done
  130.0 0.0 copy-start.1
  130.0 0.0 copy-start.3
  130.0 0.0 copy-start.2
  130.0 0.0 copy-start.4
  130.0 66.7 %shard_map.97.sums_ref = f32[2,112,2048]{2,1,0:T(8,128)} custom-call(bf16[896,1536]{1,0:T(8,128)(2,1)} %copy-done, bf16[2,1536,2048]{2,1,0:T(8,128)(2,1)} %images_hbm.3), custom_call_target="tpu_custom_call" | custom-call | tf_op jit(solution)/shard_map/pallas_call | solution.py:409
  196.7 0.0 copy-done.1
  196.7 0.1 eq.133
  196.8 1.2 convert_reduce_fusion
  198.0 0.0 copy-done.3
  198.0 0.1 broadcast_in_dim.282
  198.1 3.7 %select_reduce_fusion = s32[5120]{0:T(1024)S(1)} fusion(s32[1792]{0:T(1024)S(1)} %broadcast_in_dim.282, s32[1792]{0:T(1024)S(1)} %multiply_add_fusion), kind=kLoop, calls=%fused_computation | loop fusion | flops 27520000 | bytes 34816 | tf_op jit(solution)/shard_map/reduce_sum | solution.py:683
  201.8 0.1 reshape.63
  201.9 0.7 pad.17.table_ref
  202.6 0.1 mul.31
  202.7 0.6 reshape_add_fusion.place_ref
  203.3 0.0 copy-done.2
  203.3 0.0 copy-done.4
  203.3 0.2 select_reduce_fusion.1
  203.5 1.3 copy.41.factor_ref
  204.8 50.6 %shard_map.98 = f32[1,2,2000,128]{3,2,1,0:T(8,128)} custom-call(f32[2,112,2048]{2,1,0:T(8,128)} %shard_map.97.sums_ref, f32[16,112,4]{2,1,0:T(8,128)} %copy.41.factor_ref, s32[1,1792]{1,0:T(1,128)} %reshape_add_fusion.place_ref, s32[128,1,128]{2,1,0:T(1,128)} %pad.17.table_ref), custom_call_target="tpu_custom_call" | custom-call | tf_op jit(solution)/shard_map/pallas_call | solution.py:609
  255.4 1.7 dynamic-slice_convert_fusion
  257.1 3.0 %copy.49 = f32[1,2,2000,128]{3,2,1,0:T(8,128)} copy(f32[1,2,2000,128]{3,2,1,0:T(8,128)} %shard_map.98) | data formatting | bytes 4096000
  (4 shorter events, 0.1 us)
Async XLA Ops:
  79.4 1.4 slice-start
  128.5 1.6 copy-start
  130.0 66.7 %copy-start.1 = (s32[1,112,16,1]{1,3,2,0:T(1,128)S(1)}, s32[1,112,16,1]{1,3,2,0:T(1,128)}, u32[]{:S(2)}) copy-start(s32[1,112,16,1]{1,3,2,0:T(1,128)} %param.12) | copy-start | bytes 21508
  130.0 68.0 %copy-start.3 = (s32[1,112,16]{1,2,0:T(8,128)S(1)}, s32[1,112,16]{1,2,0:T(8,128)}, u32[]{:S(2)}) copy-start(s32[1,112,16]{1,2,0:T(8,128)} %param.13) | copy-start | bytes 21508
  130.0 73.3 %copy-start.2 = (s32[1,112,16]{1,2,0:T(8,128)S(1)}, s32[1,112,16]{1,2,0:T(8,128)}, u32[]{:S(2)}) copy-start(s32[1,112,16]{1,2,0:T(8,128)} %param.14) | copy-start | bytes 21508
  130.0 73.3 %copy-start.4 = (f32[8,4]{0,1:T(4,128)S(1)}, f32[8,4]{0,1:T(4,128)}, u32[]{:S(2)}) copy-start(f32[8,4]{0,1:T(4,128)} %param.15) | copy-start | bytes 388

commit v4 on v3

v4 whole, which is shorter than its diff:
```python
import jax
import jax.numpy as jnp
from jax import lax
from jax.experimental import pallas as pl
from jax.experimental.pallas import tpu as pltpu
from jax.sharding import PartitionSpec as P

MESH = pl.DeviceIdType.MESH
VMEM = pltpu.VMEM
DMA = pltpu.SemaphoreType.DMA
VMEM_BYTES = 60 * 1024 * 1024
RING = 4

BROWS = 2000
KEPT = 256
SLOTS = 40
MOVED = 32
ROW_SHIFT = 3
BRICK_SHIFT = 14
COARSE = 128
FINE = (64, 32, 16, 8)


tempering = 0.5
masked_logit = -1e30
contract_last = (((1,), (1,)), ((), ()))


def window_parts(prior_orient, orient_count):
    start = (prior_orient - orient_count // 8) % orient_count
    return start // COARSE, start % COARSE


def img_neighbours():
    me = lax.axis_index("img")
    z, x = me // RING, me % RING
    at = lambda other, shift: (z + other) % 2 * RING + (x + shift) % RING
    return at


def greet(others):
    barrier = pltpu.get_barrier_semaphore()
    for axis, other in others:
        pl.semaphore_signal(barrier, inc=1, device_id={axis: other}, device_id_type=MESH)
    pl.semaphore_wait(barrier, len(others))


def slot_tables(code_row, code_column, place_ref, lines, table_ref):
    segments = code_column.shape[0]
    bricks, step = table_ref.shape[0], 64
    named = jnp.right_shift(code_row[:, :segments], BRICK_SHIFT)
    ahead = lax.broadcasted_iota(jnp.int32, (1, segments), 1)

    def count_before(turn, rank):
        here = pl.ds(pl.multiple_of(turn * step, step), step)
        index = turn * step + lax.broadcasted_iota(jnp.int32, (step, 1), 0)
        same = (jnp.right_shift(code_column[here, :], BRICK_SHIFT) == named) & (index < ahead)
        return rank + jnp.sum(jnp.where(same, 1, 0), axis=0, keepdims=True)

    rank = lax.fori_loop(
        0, segments // step, count_before, jnp.zeros((1, segments), jnp.int32)
    )
    place_ref[...] = named * SLOTS + rank
    voxel = jnp.right_shift(code_row[:, :segments] & ((1 << BRICK_SHIFT) - 1), ROW_SHIFT)
    high = jnp.right_shift(voxel, 4)
    low = voxel - high * 16
    line = lax.broadcasted_iota(jnp.int32, (bricks, 1), 0)
    of_rank = jnp.where(rank == line, 1.0, 0.0).astype(jnp.bfloat16)
    table = jnp.zeros((bricks, 128), jnp.float32)
    for scale, digits in ((16.0, high), (1.0, low)):
        of_brick = jnp.where(named == line, digits.astype(jnp.float32), 0.0).astype(jnp.bfloat16)
        table = table + scale * lax.dot_general(
            of_brick, of_rank, contract_last, preferred_element_type=jnp.float32
        )
    lines[...] = table.astype(jnp.int32)

    def copy_line(brick, _):
        table_ref[brick] = lines[pl.ds(brick, 1), :]
        return 0

    lax.fori_loop(0, bricks, copy_line, 0)


def to_windows(scores_ref, prior_ref, windows_ref):
    orient_count = scores_ref.shape[0]

    def body(step, _):
        column = pl.ds(pl.multiple_of(step * 128, 128), 128)
        coarse, fine = window_parts(prior_ref[:, column], orient_count)
        rows = KEPT + sum(FINE)
        kept = scores_ref[:rows, column]
        for block in range(1, orient_count // COARSE):
            first = block * COARSE
            piece = scores_ref[first : min(first + rows, orient_count), column]
            if first + rows > orient_count:
                wrapped = scores_ref[: first + rows - orient_count, column]
                piece = jnp.concatenate([piece, wrapped], axis=0)
            kept = jnp.where(coarse == block, piece, kept)
        for size in FINE:
            rows -= size
            kept = jnp.where(fine // size % 2 == 1, kept[size : size + rows], kept[:rows])
        position = lax.broadcasted_iota(jnp.int32, (KEPT, 1), 0) - fine % FINE[-1]
        inside = (position >= 0) & (position <= 2 * (orient_count // 8))
        windows_ref[column, :] = jnp.where(inside, kept, masked_logit).T
        return 0

    lax.fori_loop(0, scores_ref.shape[1] // 128, body, 0)


def from_windows(kept_ref, prior_ref, wide_ref, rounded_ref):
    orient_count = wide_ref.shape[0]

    def body(step, _):
        column = pl.ds(pl.multiple_of(step * 128, 128), 128)
        coarse, fine = window_parts(prior_ref[:, column], orient_count)
        kept = kept_ref[column, :].astype(jnp.float32).T
        for size in FINE[::-1]:
            pad = jnp.zeros((size, 128), jnp.float32)
            kept = jnp.where(
                fine // size % 2 == 1,
                jnp.concatenate([pad, kept], axis=0),
                jnp.concatenate([kept, pad], axis=0),
            )
        kept = jnp.concatenate([kept, jnp.zeros((-kept.shape[0] % COARSE, 128), jnp.float32)], axis=0)
        blocks = orient_count // COARSE
        for block in range(blocks):
            part = jnp.zeros((COARSE, 128), jnp.float32)
            for piece in range(kept.shape[0] // COARSE):
                part = jnp.where(
                    coarse == (block - piece) % blocks,
                    kept[piece * COARSE : (piece + 1) * COARSE],
                    part,
                )
            here = slice(block * COARSE, (block + 1) * COARSE)
            wide_ref[here, column] = part
            rounded_ref[here, column] = part.astype(jnp.bfloat16)
        return 0

    lax.fori_loop(0, wide_ref.shape[1] // 128, body, 0)


def posterior_kernel(
    refs_ref, noise_ref, code_row, code_column, images_hbm,
    rounded_ref, rows_ref, place_ref, table_ref,
    images, gathered, weighted, energy, out_ref, windows_ref, kept_ref, lines,
    pair_in, chip_out, chip_in, load_sem, own_sem, send_sem, recv_sem,
    pair_send, pair_recv, chip_send, chip_recv, gat_send, gat_recv, sib_send, sib_recv,
):
    freq = lax.axis_index("freq")
    core = freq % 2
    z, y = freq // 8, freq // 2 % 4
    count = windows_ref.shape[0] // 16
    sibling = freq + 1 - 2 * core
    spots = [(dz, dy) for dz, dy in ((1, 2), (1, 1), (1, 3), (0, 2), (1, 0), (0, 1), (0, 3), (0, 0))]
    target = lambda dz, dy: (z + dz) % 2 * 8 + (y + dy) % 4 * 2 + core
    source = lambda dz, dy: (z + dz) % 2 * 8 + (y + 4 - dy) % 4 * 2 + core
    at = img_neighbours()
    rows = refs_ref.shape[1]
    load = pltpu.make_async_copy(images_hbm, images, load_sem)
    load.start()
    own = pltpu.make_async_copy(refs_ref, gathered.at[at(0, 0)], own_sem)
    own.start()
    greet(
        [("img", at(0, 1)), ("img", at(0, 3)), ("img", at(1, 0)), ("freq", sibling)]
        + [("freq", target(*spot)) for spot in spots[:-1]]
    )
    own.wait()

    def forward(number, shard, part, target, first=0, last=rows):
        some = gathered.at[shard, part, pl.ds(first, last - first)]
        copy = pltpu.make_async_remote_copy(
            src_ref=some,
            dst_ref=some,
            send_sem=send_sem.at[number],
            recv_sem=recv_sem.at[number],
            device_id={"img": target},
            device_id_type=MESH,
        )
        copy.start()
        return copy

    right, left, across = at(0, 1), at(0, 3), at(1, 0)
    mine = at(0, 0)
    own_right = [forward(0, mine, 0, right), None]
    own_left = [None, forward(1, mine, 1, left)]
    own_across = [forward(2, mine, 0, across), None]
    own_right[1] = forward(3, mine, 1, right)
    own_left[0] = forward(4, mine, 0, left)
    own_across[1] = forward(5, mine, 1, across)

    def weigh(shard, part, place, fresh, bank):
        lines = 16
        for first in range(0, rows, lines):
            value = gathered[shard, part, first : first + lines, :].astype(jnp.float32)
            scaled = value * noise_ref[...]
            here = slice(place * rows + first, place * rows + first + lines)
            weighted[here, :] = scaled.astype(jnp.bfloat16)
            squares = scaled * value
            total = squares[:, :128]
            for lane in range(128, squares.shape[1], 128):
                total = total + squares[:, lane : lane + 128]
            energy[bank, here, :] = total if fresh else energy[bank, here, :] + total

    def multiply(first, second, part, fresh, bank=0):
        weigh(first, part, 0, fresh, bank)
        weigh(second, part, 1, fresh, bank)
        if not fresh:
            half = 0.5 * jnp.sum(energy[bank], axis=1, keepdims=True)
        width = 256

        def body(step, _):
            column = pl.ds(pl.multiple_of(step * width, width), width)
            product = lax.dot_general(
                weighted[...], images[part, column, :], contract_last,
                preferred_element_type=jnp.float32,
            )
            if not fresh:
                product = product - half
            for place, shard in enumerate((first, second)):
                block = product[place * rows : (place + 1) * rows]
                there = pl.ds(pl.multiple_of(shard * rows, 16), rows)
                if fresh:
                    out_ref[there, column] = block
                else:
                    out_ref[there, column] = out_ref[there, column] + block
            return 0

        lax.fori_loop(0, images.shape[1] // width, body, 0)

    slot_tables(code_row, code_column, place_ref, lines, table_ref)
    own_right[0].wait_recv()
    next_right = forward(6, at(0, 3), 0, right)
    own_left[1].wait_recv()
    next_left = forward(7, at(0, 1), 1, left)
    extra = [forward(14, at(0, 1), 1, across, rows - MOVED), None]
    load.wait()
    own_across[0].wait_recv()
    over_right = [forward(8, at(1, 0), 0, right), None]
    over_left = [forward(9, at(1, 0), 0, left), None]
    multiply(at(0, 0), at(1, 0), 0, True)
    own_across[1].wait_recv()
    over_right[1] = forward(10, at(1, 0), 1, right, 0, rows - MOVED)
    over_left[1] = forward(11, at(1, 0), 1, left, 0, rows - MOVED)
    own_right[1].wait_recv()
    extra[1] = forward(15, at(0, 3), 1, across, rows - MOVED)
    multiply(at(0, 0), at(1, 0), 1, False)
    own_left[0].wait_recv()
    multiply(at(0, 1), at(0, 3), 0, True)
    multiply(at(0, 1), at(0, 3), 1, False)
    next_right.wait_recv()
    over_across = [forward(12, at(0, 2), 0, across), None]
    next_left.wait_recv()
    over_across[1] = forward(13, at(0, 2), 1, across)
    over_right[0].wait_recv()
    over_left[0].wait_recv()
    multiply(at(1, 1), at(1, 3), 0, True)
    over_across[0].wait_recv()
    multiply(at(0, 2), at(1, 2), 0, True, 1)
    for copy in (over_right[1], over_left[1], extra[0], extra[1]):
        copy.wait_recv()
    multiply(at(1, 1), at(1, 3), 1, False)
    over_across[1].wait_recv()
    multiply(at(0, 2), at(1, 2), 1, False, 1)
    for copy in (
        own_right + own_left + own_across + [next_right, next_left]
        + over_right + over_left + over_across + extra
    ):
        copy.wait_send()
    prior_ref = code_row.at[:, pl.ds(code_column.shape[0], out_ref.shape[1])]
    to_windows(out_ref, prior_ref, windows_ref)
    block_lines = lambda block: pl.ds(pl.multiple_of(block * count, 16), count)

    def send(src, dst, send_sem, recv_sem, other):
        copy = pltpu.make_async_remote_copy(
            src_ref=src, dst_ref=dst, send_sem=send_sem, recv_sem=recv_sem,
            device_id={"freq": other}, device_id_type=MESH,
        )
        copy.start()
        return copy

    pairs = []
    for n, spot in enumerate(spots):
        block = target(*spot) + 1 - 2 * core
        pairs.append(
            send(windows_ref.at[block_lines(block)], pair_in.at[n], pair_send.at[n], pair_recv.at[n], sibling)
        )
    chips = []
    for n, spot in enumerate(spots):
        pairs[n].wait_recv()
        total = windows_ref[block_lines(target(*spot)), :] + pair_in[n]
        if n == 7:
            break
        chip_out[n] = total
        chips.append(
            send(chip_out.at[n], chip_in.at[n], chip_send.at[n], chip_recv.at[n], target(*spot))
        )
    chip_out[7] = total
    scores = chip_out[7]
    for n in range(7):
        chips[6 - n].wait_recv()
        scores = scores + chip_in[6 - n]
    inside = scores > 0.5 * masked_logit
    logits = jnp.where(inside, tempering * scores, masked_logit)
    raised = jnp.where(inside, jnp.exp(logits - jnp.max(logits, axis=1, keepdims=True)), 0.0)
    result = raised / jnp.sum(raised, axis=1, keepdims=True)
    kept_ref[block_lines(freq), :] = result.astype(jnp.bfloat16)
    gathers, relays = [], []
    for n, spot in enumerate(spots[:-1]):
        here = kept_ref.at[block_lines(freq)]
        gathers.append(send(here, here, gat_send.at[n], gat_recv.at[n], target(*spot)))
    here = kept_ref.at[block_lines(freq)]
    relays.append(send(here, here, sib_send.at[7], sib_recv.at[7], sibling))
    for n in range(6, -1, -1):
        gathers[n].wait_recv()
        here = kept_ref.at[block_lines(source(*spots[n]))]
        relays.append(send(here, here, sib_send.at[n], sib_recv.at[n], sibling))
    for copy in relays:
        copy.wait_recv()
    for copy in pairs + chips + gathers + relays:
        copy.wait_send()
    from_windows(kept_ref, prior_ref, out_ref, rounded_ref)
    share = rows_ref.shape[0]
    rows_ref[...] = out_ref[pl.ds(pl.multiple_of(freq * share, 8), share), :]


def posteriors(
    references, noise_weight, code_row, code_column, images, image_groups, freq_groups
):
    parts, rows, freqs = references.shape
    count = images.shape[1]
    orients, segments = image_groups * rows, code_column.shape[0]
    bricks = image_groups * freq_groups
    share = count // freq_groups
    return pl.pallas_call(
        posterior_kernel,
        out_shape=(
            jax.ShapeDtypeStruct((orients, count), jnp.bfloat16),
            jax.ShapeDtypeStruct((orients * share // count, count), jnp.float32),
            jax.ShapeDtypeStruct((1, segments), jnp.int32),
            jax.ShapeDtypeStruct((bricks, 1, 128), jnp.int32),
        ),
        in_specs=[pl.BlockSpec(memory_space=VMEM)] * 4 + [pl.BlockSpec(memory_space=pl.ANY)],
        out_specs=[pl.BlockSpec(memory_space=VMEM)] * 4,
        scratch_shapes=[
            VMEM(images.shape, jnp.bfloat16),
            VMEM((image_groups, parts, rows, freqs), jnp.bfloat16),
            VMEM((2 * rows, freqs), jnp.bfloat16),
            VMEM((2, 2 * rows, 128), jnp.float32),
            VMEM((orients, count), jnp.float32),
            VMEM((count, KEPT), jnp.float32),
            VMEM((count, KEPT), jnp.bfloat16),
            VMEM((bricks, 128), jnp.int32),
        ]
        + [VMEM((8, share, KEPT), jnp.float32) for _ in range(3)]
        + [DMA(()), DMA(()), DMA((16,)), DMA((16,))]
        + [DMA((8,)) for _ in range(8)],
        compiler_params=pltpu.CompilerParams(
            collective_id=0, has_side_effects=True, vmem_limit_bytes=VMEM_BYTES
        ),
    )(references, noise_weight.reshape(1, freqs), code_row, code_column, images)


def volume_kernel(
    rounded_ref, code_column, taps_ref, place_ref, table_ref, images_hbm, out_ref,
    images, lhs, part, first_in, side_in, half_in, near_in, last_in, extra_in, sums_ref,
    values, packed, arrived, lines_in, members, terms, factor_ref,
    load_sem, group_send, group_recv, send_sem, recv_sem, line_send, line_recv, own_sem,
):
    groups, wide = 8, 16
    img, freq = lax.axis_index("img"), lax.axis_index("freq")
    barrier = pltpu.get_barrier_semaphore()
    at = img_neighbours()
    rows, freqs = sums_ref.shape[1:]
    loads = []
    for n in range(2):
        loads.append(pltpu.make_async_copy(images_hbm.at[n], images.at[n], load_sem.at[n]))
        loads[-1].start()
    right, left, across = at(0, 1), at(0, 3), at(1, 0)

    def everyone(visit):
        def outer(di, _):
            def inner(df, _):
                @pl.when((di > 0) | (df > 0))
                def _():
                    visit(di, (img + di) % groups, (freq + df) % wide)

                return 0

            return lax.fori_loop(0, wide, inner, 0)

        lax.fori_loop(0, groups, outer, 0)

    everyone(
        lambda di, to_img, to_freq: pl.semaphore_signal(
            barrier, inc=1, device_id={"img": to_img, "freq": to_freq}, device_id_type=MESH
        )
    )

    def multiply(first, second, n):
        for place, (other, shift) in enumerate((first, second)):
            there = pl.ds(pl.multiple_of(at(other, shift) * rows, 16), rows)
            lhs[place * rows : (place + 1) * rows, :] = rounded_ref[there, :]
        width = 256

        def body(step, _):
            column = pl.ds(pl.multiple_of(step * width, width), width)
            product = jnp.dot(
                lhs[...], images[n, :, column], preferred_element_type=jnp.float32
            ).astype(jnp.bfloat16)
            for place, (other, shift) in enumerate((first, second)):
                part[other * 4 + shift, n, :, column] = product[place * rows : (place + 1) * rows]
            return 0

        lax.fori_loop(0, freqs // width, body, 0)

    copies = []

    def send(src, dst, target):
        number = len(copies)
        copy = pltpu.make_async_remote_copy(
            src_ref=src, dst_ref=dst, send_sem=group_send.at[number], recv_sem=group_recv.at[number],
            device_id={"img": target}, device_id_type=MESH,
        )
        copy.start()
        copies.append(copy)
        return copy

    def combine(dst, sources, count=rows):
        lines = 16

        def body(step, _):
            here = pl.ds(pl.multiple_of(step * lines, lines), lines)
            total = sources[0][here, :].astype(jnp.float32)
            for source in sources[1:]:
                total = total + source[here, :].astype(jnp.float32)
            dst[here, :] = total.astype(dst.dtype)
            return 0

        lax.fori_loop(0, count // lines, body, 0)

    stay = rows - MOVED
    kept, moved = pl.ds(0, stay), pl.ds(stay, MOVED)
    first, sides, near, extra = [], [[], []], [[None, None], [None, None]], []
    for n in range(2):
        loads[n].wait()
        multiply((1, 1), (1, 3), n)
        if n == 0:
            pl.semaphore_wait(barrier, groups * wide - 1)
        some = pl.ds(0, rows) if n == 0 else kept
        for way, (here, there) in enumerate(((5, right), (7, left))):
            sides[way].append(send(part.at[here, n, some], side_in.at[way, n, some], there))
        multiply((1, 2), (0, 2), n)
        first.append(send(part.at[6, n], first_in.at[n], across))
    for way, here in enumerate((5, 7)):
        extra.append(send(part.at[here, 1, moved], extra_in.at[way], across))
    me = img * wide + freq

    def send_line(di, to_img, to_freq):
        pltpu.make_async_remote_copy(
            src_ref=table_ref.at[to_img * wide + to_freq],
            dst_ref=lines_in.at[me],
            send_sem=line_send,
            recv_sem=line_recv,
            device_id={"img": to_img, "freq": to_freq},
            device_id_type=MESH,
        ).start()

    everyone(send_line)
    lines_in[me] = table_ref[me]

    for n in range(2):
        multiply((0, 1), (0, 3), n)
    halves = []
    first[0].wait_recv()
    combine(part.at[2, 0], [part.at[2, 0], first_in.at[0]])
    halves.append(send(part.at[2, 0], half_in.at[0], left))
    for n in range(2):
        multiply((1, 0), (0, 0), n)
    first[1].wait_recv()
    combine(part.at[2, 1], [part.at[2, 1], first_in.at[1]])
    halves.append(send(part.at[2, 1], half_in.at[1], right))
    near[0][0] = send(part.at[1, 0], near_in.at[0, 0], right)
    for way, here in enumerate((1, 3)):
        extra[way].wait_recv()
        some = part.at[here, 1, moved]
        combine(some, [some, extra_in.at[way]], MOVED)
    near[1][1] = send(part.at[3, 1], near_in.at[1, 1], left)
    phases, tap_count = taps_ref.shape
    for q in range(factor_ref.shape[0]):
        kernel = code_column[q * rows : (q + 1) * rows, :] & ((1 << ROW_SHIFT) - 1)
        for tap in range(tap_count):
            factor = jnp.zeros((rows, 1), jnp.float32)
            for phase in range(phases):
                factor = jnp.where(kernel == phase, taps_ref[phase, tap], factor)
            factor_ref[q, :, tap : tap + 1] = factor
    last = []
    for n in range(2):
        sides[0][n].wait_recv()
        sides[1][n].wait_recv()
        combine(
            part.at[4, n], [part.at[4, n], side_in.at[0, n], side_in.at[1, n]],
            rows if n == 0 else stay,
        )
        last.append(send(part.at[4, n], last_in.at[n], across))
    halves[0].wait_recv()
    combine(part.at[3, 0], [part.at[3, 0], half_in.at[0]])
    near[1][0] = send(part.at[3, 0], near_in.at[1, 0], left)
    halves[1].wait_recv()
    combine(part.at[1, 1], [part.at[1, 1], half_in.at[1]])
    near[0][1] = send(part.at[1, 1], near_in.at[0, 1], right)
    for n in range(2):
        near[0][n].wait_recv()
        near[1][n].wait_recv()
        last[n].wait_recv()
        combine(
            sums_ref.at[n], [part.at[0, n], near_in.at[0, n], near_in.at[1, n], last_in.at[n]]
        )
    for copy in copies:
        copy.wait_send()
    slots = packed.shape[1] // 2
    segments = values.shape[0]
    lanes = freqs // (segments // rows)
    lane = lax.broadcasted_iota(jnp.int32, (rows, lanes), 1)
    for q in range(segments // rows):
        for part in range(2):
            value = sums_ref[part, :, q * lanes : (q + 1) * lanes]
            shifted = [
                jnp.where(lane < lanes - 1, pltpu.roll(value, lanes - 1, 1), 0.0),
                value,
                jnp.where(lane >= 1, pltpu.roll(value, 1, 1), 0.0),
                jnp.where(lane >= 2, pltpu.roll(value, 2, 1), 0.0),
            ]
            result = factor_ref[q, :, 0:1] * shifted[0]
            for tap in range(1, 4):
                result = result + factor_ref[q, :, tap : tap + 1] * shifted[tap]
            values[q * rows : (q + 1) * rows, part * lanes : (part + 1) * lanes] = result.astype(
                jnp.bfloat16
            )
    def send_group(di, _):
        to_img = (img + di) % groups
        some = wide // 2

        def pack(half, _):
            base = (to_img * wide + half * some) * slots
            slot = base + lax.broadcasted_iota(jnp.int32, (some * slots, 1), 0)
            found = jnp.zeros((some * slots, 2 * lanes), jnp.float32)
            step = 256
            for first in range(0, segments, step):
                hit = jnp.where(place_ref[:, first : first + step] == slot, 1.0, 0.0)
                found = found + jnp.dot(
                    hit.astype(jnp.bfloat16), values[first : first + step, :],
                    preferred_element_type=jnp.float32,
                )
            for brick in range(some):
                block = found[brick * slots : (brick + 1) * slots]
                packed[to_img * wide + half * some + brick] = jnp.concatenate(
                    [block[:, :lanes], block[:, lanes:]], axis=0
                ).astype(jnp.bfloat16)
            return 0

        lax.fori_loop(0, 2, pack, 0)

        def inner(df, _):
            to_freq = (freq + df) % wide

            @pl.when((di > 0) | (df > 0))
            def _():
                pltpu.make_async_remote_copy(
                    src_ref=packed.at[to_img * wide + to_freq],
                    dst_ref=arrived.at[me],
                    send_sem=send_sem,
                    recv_sem=recv_sem.at[di],
                    device_id={"img": to_img, "freq": to_freq},
                    device_id_type=MESH,
                ).start()

            return 0

        return lax.fori_loop(0, wide, inner, 0)

    lax.fori_loop(0, groups, send_group, 0)
    own = pltpu.make_async_copy(packed.at[me], arrived.at[me], own_sem)
    own.start()
    most = pl.ds(0, groups * wide - 1)
    pltpu.make_async_copy(lines_in.at[most], lines_in.at[most], line_recv).wait()
    pltpu.make_async_copy(table_ref.at[most], table_ref.at[most], line_send).wait()
    place = lax.broadcasted_iota(jnp.int32, (1, 128), 1)
    chunks = wide * slots // 128
    row_step = 400
    held = members.shape[0]

    def make_members(di, _):
        group = (img + groups - di) % groups
        row_lines = [jnp.zeros((1, 128), jnp.int32) for _ in range(chunks)]
        for member in range(wide):
            line = lines_in[group * wide + member]
            chunk, first = member * slots // 128, member * slots % 128
            turned = pltpu.roll(line, first, 1) if first else line
            row_lines[chunk] = jnp.where(
                (place >= first) & (place < first + slots), turned, row_lines[chunk]
            )
            if first + slots > 128:
                row_lines[chunk + 1] = jnp.where(
                    place < first + slots - 128, turned, row_lines[chunk + 1]
                )
        row_lines = jnp.concatenate(row_lines, axis=1)

        def fill(step, _):
            first = pl.multiple_of(step * 16, 16)
            voxel = first + lax.broadcasted_iota(jnp.int32, (16, 1), 0)
            members[di % held, pl.ds(first, 16), :] = jnp.where(row_lines == voxel, 1.0, 0.0).astype(
                jnp.bfloat16
            )
            return 0

        return lax.fori_loop(0, BROWS // 16, fill, 0)

    lax.fori_loop(0, held, make_members, 0)
    for di in range(groups):
        group = (img + groups - di) % groups
        count = wide - 1 if di == 0 else wide
        some = pl.ds(0, count)
        pltpu.make_async_copy(arrived.at[some], arrived.at[some], recv_sem.at[di]).wait()
        if di == 0:
            own.wait()
        for pair in range(wide // 2):
            blocks = [
                arrived[group * wide + 2 * pair + n].astype(jnp.float32) for n in range(2)
            ]
            for part in range(2):
                both = [block[part * slots : (part + 1) * slots] for block in blocks]
                terms[2 * pair * slots : 2 * (pair + 1) * slots, part * lanes : (part + 1) * lanes] = (
                    jnp.concatenate(both, axis=0).astype(jnp.bfloat16)
                )

        def add(step, _):
            here = pl.ds(pl.multiple_of(step * row_step, 16), row_step)
            found = jnp.dot(members[di % held, here, :], terms[...], preferred_element_type=jnp.float32)
            if di > 0:
                found = found + jnp.concatenate([out_ref[0, 0, here, :], out_ref[0, 1, here, :]], axis=1)
            out_ref[0, 0, here, :] = found[:, :lanes]
            out_ref[0, 1, here, :] = found[:, lanes:]
            return 0

        lax.fori_loop(0, BROWS // row_step, add, 0)
        if di + held < groups:
            make_members(di + held, 0)
    pltpu.make_async_copy(packed.at[most], packed.at[most], send_sem).wait()


def back_projected(rounded, images, code_column, kernel_taps, places, table, image_groups):
    rows = rounded.shape[0] // image_groups
    parts, count, freqs = images.shape
    block = (parts, rows, freqs)
    bricks, segments, lanes = table.shape[0], places.shape[1], 128
    return pl.pallas_call(
        volume_kernel,
        out_shape=jax.ShapeDtypeStruct((1, parts, BROWS, lanes), jnp.float32),
        in_specs=[pl.BlockSpec(memory_space=VMEM)] * 2
        + [pl.BlockSpec(memory_space=pltpu.SMEM)]
        + [pl.BlockSpec(memory_space=VMEM)] * 2
        + [pl.BlockSpec(memory_space=pl.ANY)],
        out_specs=pl.BlockSpec(memory_space=VMEM),
        scratch_shapes=[
            VMEM(images.shape, jnp.bfloat16),
            VMEM((2 * rows, count), jnp.bfloat16),
            VMEM((image_groups, *block), jnp.bfloat16),
            VMEM(block, jnp.bfloat16),
            VMEM((2, *block), jnp.bfloat16),
            VMEM(block, jnp.bfloat16),
            VMEM((2, *block), jnp.bfloat16),
            VMEM(block, jnp.bfloat16),
            VMEM((2, MOVED, freqs), jnp.bfloat16),
            VMEM(block, jnp.float32),
            VMEM((segments, 2 * lanes), jnp.bfloat16),
            VMEM((bricks, 2 * SLOTS, lanes), jnp.bfloat16),
            VMEM((bricks, 2 * SLOTS, lanes), jnp.bfloat16),
            VMEM((bricks, 1, 128), jnp.int32),
            VMEM((4, BROWS, 16 * SLOTS), jnp.bfloat16),
            VMEM((16 * SLOTS, 2 * lanes), jnp.bfloat16),
            VMEM((segments // rows, rows, kernel_taps.shape[1]), jnp.float32),
            DMA((2,)),
            DMA((16,)),
            DMA((16,)),
            DMA(()),
            DMA((8,)),
            DMA(()),
            DMA(()),
            DMA(()),
        ],
        compiler_params=pltpu.CompilerParams(
            collective_id=2, has_side_effects=True, vmem_limit_bytes=VMEM_BYTES
        ),
    )(rounded, code_column, kernel_taps, places, table, images)


def on_device(
    images,
    references,
    noise_weight,
    prior_orient,
    segment_brick,
    segment_row,
    segment_kernel,
    kernel_taps,
):
    image_groups = lax.axis_size("img")
    freq_groups = lax.axis_size("freq")
    local_orients = references.shape[1]
    segment_blocks = segment_row.shape[2]
    codes = (segment_brick[..., 0] << BRICK_SHIFT) + (segment_row << ROW_SHIFT) + segment_kernel
    codes = codes.reshape(local_orients, segment_blocks).T.reshape(-1)
    code_row = jnp.concatenate([codes, prior_orient])[None, :]
    code_column = codes[:, None]
    rounded, own_rows, places, table = posteriors(
        references, noise_weight, code_row, code_column, images, image_groups, freq_groups
    )
    volume = back_projected(
        rounded, images, code_column, kernel_taps, places, table, image_groups
    )
    return (own_rows, volume)


def solution(mesh):
    in_specs = (
        P(None, "img", "freq"),
        P(None, "img", "freq"),
        P("freq"),
        P("img"),
        P("freq", "img", None, None),
        P("freq", "img", None),
        P("freq", "img", None),
        P(),
    )
    out_specs = (P("freq", "img"), P(("img", "freq"), None, None, None))
    return jax.shard_map(
        on_device, mesh=mesh, in_specs=in_specs, out_specs=out_specs, check_vma=False
    )
```

time: 262 us -> 216 us (0.82)
  the two profiles are of different devices: /device:TPU:1 before, /device:TPU:27 now
where the time goes in v4:
time: 216 us
  Pallas kernels  207 us (96%)
  local copies, waits for them, and re-layouts  7.02 us (3%)
    pallas_call x1, Pallas kernels, back_projected(): pl.pallas_call(volume_kernel, out_shape=jax.ShapeDtypeStruct((1, parts, B...  117 us
    pallas_call x1, Pallas kernels, posteriors(): pl.pallas_call(posterior_kernel, out_shape=(jax.ShapeDtypeStruct((orients...  90.1 us
    unnamed x5, local copies, waits for them, and re-layouts  5.09 us

profile of v4, /device:TPU:27, one launch (start us, length us, event | category | flops | bytes accessed | tf_op | source)
XLA Modules:
  0.0 216.0 jit_solution(14766898388468899635)
XLA Ops:
  0.6 1.4 copy.15.taps_ref
  2.0 0.7 fusion.1
  2.7 0.1 reshape.29
  2.8 0.7 pad_add_fusion
  3.5 0.6 broadcast_in_dim.3.code_row
  4.1 1.2 broadcast_in_dim_reshape.4.code_column
  5.4 90.1 %shard_map.95 = (bf16[896,1536]{1,0:T(8,128)(2,1)}, f32[56,1536]{1,0:T(8,128)}, s32[1,1792]{1,0:T(1,128)}, s32[128,1,128]{2,1,0:T(1,128)}) custom-call(bf16[2,112,2048]{2,1,0:T(8,128)(2,1)} %refs_ref.1, f32[1,2048]{1,0:T(1,128)} %bitcast.12, s32[1,3328]{1,0:T(1,128)} %broadcast_in_dim.3.code_row, s32[1792,1]{1,0:T(8,128)} %broadcast_in_dim_reshape.4.code_column, ...), custom_call_target="tpu_custom_call" | custom-call | tf_op jit(solution)/shard_map/pallas_call | solution.py:334
  95.5 0.0 copy-start
  95.5 116.7 %shard_map.96 = f32[1,2,2000,128]{3,2,1,0:T(8,128)} custom-call(bf16[896,1536]{1,0:T(8,128)(2,1)} %get-tuple-element.7.rounded_ref, s32[1792,1]{1,0:T(8,128)} %broadcast_in_dim_reshape.4.code_column, f32[8,4]{1,0:T(8,128)} %copy.15.taps_ref, s32[1,1792]{1,0:T(1,128)} %get-tuple-element.8.place_ref, s32[128,1,128]{2,1,0:T(1,128)} %get-tuple-element.9.table_ref, ...), custom_call_target="tpu_custom_call" | custom-call | tf_op jit(solution)/shard_map/pallas_call | solution.py:656
  212.2 0.0 copy-done
  212.2 0.7 copy.18
  213.0 3.0 %copy.19 = f32[1,2,2000,128]{3,2,1,0:T(8,128)} copy(f32[1,2,2000,128]{3,2,1,0:T(8,128)} %shard_map.96) | data formatting | bytes 4096000
Async XLA Ops:
  95.5 116.7 %copy-start = (f32[56,1536]{1,0:T(8,128)S(1)}, f32[56,1536]{1,0:T(8,128)}, u32[]{:S(2)}) copy-start(f32[56,1536]{1,0:T(8,128)} %get-tuple-element.12) | copy-start | bytes 1032196

commit v5 on v4

--- a/solution.py
+++ b/solution.py
@@ -502,6 +502,44 @@
             rows if n == 0 else stay,
         )
         last.append(send(part.at[4, n], last_in.at[n], across))
+    slots = packed.shape[1] // 2
+    order = (0, 1, 2, 3, 4, 5, 6, 7)
+    most = pl.ds(0, groups * wide - 1)
+    place = lax.broadcasted_iota(jnp.int32, (1, 128), 1)
+    chunks = wide * slots // 128
+    row_step = 1008
+    held = members.shape[0]
+
+    def make_members(turn):
+        group = (img + groups - order[turn]) % groups
+        row_lines = [jnp.zeros((1, 128), jnp.int32) for _ in range(chunks)]
+        for member in range(wide):
+            line = lines_in[group * wide + member]
+            chunk, first = member * slots // 128, member * slots % 128
+            turned = pltpu.roll(line, first, 1) if first else line
+            row_lines[chunk] = jnp.where(
+                (place >= first) & (place < first + slots), turned, row_lines[chunk]
+            )
+            if first + slots > 128:
+                row_lines[chunk + 1] = jnp.where(
+                    place < first + slots - 128, turned, row_lines[chunk + 1]
+                )
+        row_lines = jnp.concatenate(row_lines, axis=1)
+
+        def fill(step, _):
+            first = pl.multiple_of(step * 16, 16)
+            voxel = first + lax.broadcasted_iota(jnp.int32, (16, 1), 0)
+            members[turn % held, pl.ds(first, 16), :] = jnp.where(row_lines == voxel, 1.0, 0.0).astype(
+                jnp.bfloat16
+            )
+            return 0
+
+        lax.fori_loop(0, BROWS // 16, fill, 0)
+
+    pltpu.make_async_copy(lines_in.at[most], lines_in.at[most], line_recv).wait()
+    pltpu.make_async_copy(table_ref.at[most], table_ref.at[most], line_send).wait()
+    for turn in range(held):
+        make_members(turn)
     halves[0].wait_recv()
     combine(part.at[3, 0], [part.at[3, 0], half_in.at[0]])
     near[1][0] = send(part.at[3, 0], near_in.at[1, 0], left)
@@ -517,7 +555,6 @@
         )
     for copy in copies:
         copy.wait_send()
-    slots = packed.shape[1] // 2
     segments = values.shape[0]
     lanes = freqs // (segments // rows)
     lane = lax.broadcasted_iota(jnp.int32, (rows, lanes), 1)
@@ -536,7 +573,7 @@
             values[q * rows : (q + 1) * rows, part * lanes : (part + 1) * lanes] = result.astype(
                 jnp.bfloat16
             )
-    def send_group(di, _):
+    def send_group(di):
         to_img = (img + di) % groups
         some = wide // 2
 
@@ -576,52 +613,17 @@
 
             return 0
 
-        return lax.fori_loop(0, wide, inner, 0)
-
-    lax.fori_loop(0, groups, send_group, 0)
-    own = pltpu.make_async_copy(packed.at[me], arrived.at[me], own_sem)
-    own.start()
-    most = pl.ds(0, groups * wide - 1)
-    pltpu.make_async_copy(lines_in.at[most], lines_in.at[most], line_recv).wait()
-    pltpu.make_async_copy(table_ref.at[most], table_ref.at[most], line_send).wait()
-    place = lax.broadcasted_iota(jnp.int32, (1, 128), 1)
-    chunks = wide * slots // 128
-    row_step = 400
-    held = members.shape[0]
-
-    def make_members(di, _):
-        group = (img + groups - di) % groups
-        row_lines = [jnp.zeros((1, 128), jnp.int32) for _ in range(chunks)]
-        for member in range(wide):
-            line = lines_in[group * wide + member]
-            chunk, first = member * slots // 128, member * slots % 128
-            turned = pltpu.roll(line, first, 1) if first else line
-            row_lines[chunk] = jnp.where(
-                (place >= first) & (place < first + slots), turned, row_lines[chunk]
-            )
-            if first + slots > 128:
-                row_lines[chunk + 1] = jnp.where(
-                    place < first + slots - 128, turned, row_lines[chunk + 1]
-                )
-        row_lines = jnp.concatenate(row_lines, axis=1)
-
-        def fill(step, _):
-            first = pl.multiple_of(step * 16, 16)
-            voxel = first + lax.broadcasted_iota(jnp.int32, (16, 1), 0)
-            members[di % held, pl.ds(first, 16), :] = jnp.where(row_lines == voxel, 1.0, 0.0).astype(
-                jnp.bfloat16
-            )
-            return 0
-
-        return lax.fori_loop(0, BROWS // 16, fill, 0)
-
-    lax.fori_loop(0, held, make_members, 0)
-    for di in range(groups):
+        lax.fori_loop(0, wide, inner, 0)
+
+    def take_group(turn):
+        di = order[turn]
         group = (img + groups - di) % groups
         count = wide - 1 if di == 0 else wide
         some = pl.ds(0, count)
         pltpu.make_async_copy(arrived.at[some], arrived.at[some], recv_sem.at[di]).wait()
         if di == 0:
+            own = pltpu.make_async_copy(packed.at[me], arrived.at[me], own_sem)
+            own.start()
             own.wait()
         for pair in range(wide // 2):
             blocks = [
@@ -633,18 +635,22 @@
                     jnp.concatenate(both, axis=0).astype(jnp.bfloat16)
                 )
 
-        def add(step, _):
-            here = pl.ds(pl.multiple_of(step * row_step, 16), row_step)
-            found = jnp.dot(members[di % held, here, :], terms[...], preferred_element_type=jnp.float32)
-            if di > 0:
+        for here in (slice(0, row_step), slice(row_step, BROWS)):
+            found = jnp.dot(
+                members[turn % held, here, :], terms[...], preferred_element_type=jnp.float32
+            )
+            if turn > 0:
                 found = found + jnp.concatenate([out_ref[0, 0, here, :], out_ref[0, 1, here, :]], axis=1)
             out_ref[0, 0, here, :] = found[:, :lanes]
             out_ref[0, 1, here, :] = found[:, lanes:]
-            return 0
-
-        lax.fori_loop(0, BROWS // row_step, add, 0)
-        if di + held < groups:
-            make_members(di + held, 0)
+        if turn + held < groups:
+            make_members(turn + held)
+
+    for turn in range(groups + 8):
+        if turn < groups:
+            send_group(order[turn])
+        if turn >= 8:
+            take_group(turn - 8)
     pltpu.make_async_copy(packed.at[most], packed.at[most], send_sem).wait()
 
 

time: 216 us -> 209 us (0.968)
  the two profiles are of different devices: /device:TPU:27 before, /device:TPU:1 now
where the time goes in v5:
time: 209 us
  Pallas kernels  200 us (96%)
  local copies, waits for them, and re-layouts  7.02 us (3%)
    pallas_call x1, Pallas kernels, back_projected(): pl.pallas_call(volume_kernel, out_shape=jax.ShapeDtypeStruct((1, parts, B...  106 us
    pallas_call x1, Pallas kernels, posteriors(): pl.pallas_call(posterior_kernel, out_shape=(jax.ShapeDtypeStruct((orients...  94 us
    unnamed x5, local copies, waits for them, and re-layouts  5.09 us

profile of v5, /device:TPU:1, one launch (start us, length us, event | category | flops | bytes accessed | tf_op | source)
XLA Modules:
  0.0 208.9 jit_solution(9978499566683184061)
XLA Ops:
  0.6 1.4 copy.15.taps_ref
  2.0 0.7 fusion.1
  2.7 0.1 reshape.29
  2.8 0.7 pad_add_fusion
  3.5 0.6 broadcast_in_dim.3.code_row
  4.1 1.2 broadcast_in_dim_reshape.4.code_column
  5.4 94.0 %shard_map.95 = (bf16[896,1536]{1,0:T(8,128)(2,1)}, f32[56,1536]{1,0:T(8,128)}, s32[1,1792]{1,0:T(1,128)}, s32[128,1,128]{2,1,0:T(1,128)}) custom-call(bf16[2,112,2048]{2,1,0:T(8,128)(2,1)} %refs_ref.1, f32[1,2048]{1,0:T(1,128)} %bitcast.12, s32[1,3328]{1,0:T(1,128)} %broadcast_in_dim.3.code_row, s32[1792,1]{1,0:T(8,128)} %broadcast_in_dim_reshape.4.code_column, ...), custom_call_target="tpu_custom_call" | custom-call | tf_op jit(solution)/shard_map/pallas_call | solution.py:334
  99.4 0.0 copy-start
  99.4 105.8 %shard_map.96 = f32[1,2,2000,128]{3,2,1,0:T(8,128)} custom-call(bf16[896,1536]{1,0:T(8,128)(2,1)} %get-tuple-element.7.rounded_ref, s32[1792,1]{1,0:T(8,128)} %broadcast_in_dim_reshape.4.code_column, f32[8,4]{1,0:T(8,128)} %copy.15.taps_ref, s32[1,1792]{1,0:T(1,128)} %get-tuple-element.8.place_ref, s32[128,1,128]{2,1,0:T(1,128)} %get-tuple-element.9.table_ref, ...), custom_call_target="tpu_custom_call" | custom-call | tf_op jit(solution)/shard_map/pallas_call | solution.py:662
  205.2 0.0 copy-done
  205.2 0.7 copy.18
  205.9 3.0 %copy.19 = f32[1,2,2000,128]{3,2,1,0:T(8,128)} copy(f32[1,2,2000,128]{3,2,1,0:T(8,128)} %shard_map.96) | data formatting | bytes 4096000
Async XLA Ops:
  99.4 105.8 %copy-start = (f32[56,1536]{1,0:T(8,128)S(1)}, f32[56,1536]{1,0:T(8,128)}, u32[]{:S(2)}) copy-start(f32[56,1536]{1,0:T(8,128)} %get-tuple-element.12) | copy-start | bytes 1032196

commit v6 on v5

--- a/solution.py
+++ b/solution.py
@@ -546,20 +546,12 @@
     halves[1].wait_recv()
     combine(part.at[1, 1], [part.at[1, 1], half_in.at[1]])
     near[0][1] = send(part.at[1, 1], near_in.at[0, 1], right)
-    for n in range(2):
-        near[0][n].wait_recv()
-        near[1][n].wait_recv()
-        last[n].wait_recv()
-        combine(
-            sums_ref.at[n], [part.at[0, n], near_in.at[0, n], near_in.at[1, n], last_in.at[n]]
-        )
-    for copy in copies:
-        copy.wait_send()
     segments = values.shape[0]
     lanes = freqs // (segments // rows)
     lane = lax.broadcasted_iota(jnp.int32, (rows, lanes), 1)
-    for q in range(segments // rows):
-        for part in range(2):
+
+    def spread(part):
+        for q in range(segments // rows):
             value = sums_ref[part, :, q * lanes : (q + 1) * lanes]
             shifted = [
                 jnp.where(lane < lanes - 1, pltpu.roll(value, lanes - 1, 1), 0.0),
@@ -573,6 +565,17 @@
             values[q * rows : (q + 1) * rows, part * lanes : (part + 1) * lanes] = result.astype(
                 jnp.bfloat16
             )
+
+    for n in range(2):
+        near[0][n].wait_recv()
+        near[1][n].wait_recv()
+        last[n].wait_recv()
+        combine(
+            sums_ref.at[n], [part.at[0, n], near_in.at[0, n], near_in.at[1, n], last_in.at[n]]
+        )
+        spread(n)
+    for copy in copies:
+        copy.wait_send()
     def send_group(di):
         to_img = (img + di) % groups
         some = wide // 2

time: 209 us -> 208 us (level)
  no operation moved by 1% of the time
where the time goes in v6:
time: 208 us; the launch traced here: 207 us
  Pallas kernels  198 us (95%)
  local copies, waits for them, and re-layouts  7.02 us (3%)
    pallas_call x1, Pallas kernels, back_projected(): pl.pallas_call(volume_kernel, out_shape=jax.ShapeDtypeStruct((1, parts, B...  104 us
    pallas_call x1, Pallas kernels, posteriors(): pl.pallas_call(posterior_kernel, out_shape=(jax.ShapeDtypeStruct((orients...  94 us
    unnamed x5, local copies, waits for them, and re-layouts  5.09 us

profile of v6, /device:TPU:1, one launch (start us, length us, event | category | flops | bytes accessed | tf_op | source)
XLA Modules:
  0.0 207.0 jit_solution(17571406139849277108)
XLA Ops:
  0.6 1.4 copy.15.taps_ref
  2.0 0.7 fusion.1
  2.7 0.1 reshape.29
  2.8 0.7 pad_add_fusion
  3.5 0.6 broadcast_in_dim.3.code_row
  4.1 1.2 broadcast_in_dim_reshape.4.code_column
  5.4 94.0 %shard_map.95 = (bf16[896,1536]{1,0:T(8,128)(2,1)}, f32[56,1536]{1,0:T(8,128)}, s32[1,1792]{1,0:T(1,128)}, s32[128,1,128]{2,1,0:T(1,128)}) custom-call(bf16[2,112,2048]{2,1,0:T(8,128)(2,1)} %refs_ref.1, f32[1,2048]{1,0:T(1,128)} %bitcast.12, s32[1,3328]{1,0:T(1,128)} %broadcast_in_dim.3.code_row, s32[1792,1]{1,0:T(8,128)} %broadcast_in_dim_reshape.4.code_column, ...), custom_call_target="tpu_custom_call" | custom-call | tf_op jit(solution)/shard_map/pallas_call | solution.py:334
  99.4 0.0 copy-start
  99.4 103.8 %shard_map.96 = f32[1,2,2000,128]{3,2,1,0:T(8,128)} custom-call(bf16[896,1536]{1,0:T(8,128)(2,1)} %get-tuple-element.7.rounded_ref, s32[1792,1]{1,0:T(8,128)} %broadcast_in_dim_reshape.4.code_column, f32[8,4]{1,0:T(8,128)} %copy.15.taps_ref, s32[1,1792]{1,0:T(1,128)} %get-tuple-element.8.place_ref, s32[128,1,128]{2,1,0:T(1,128)} %get-tuple-element.9.table_ref, ...), custom_call_target="tpu_custom_call" | custom-call | tf_op jit(solution)/shard_map/pallas_call | solution.py:665
  203.2 0.0 copy-done
  203.2 0.7 copy.18
  204.0 3.0 %copy.19 = f32[1,2,2000,128]{3,2,1,0:T(8,128)} copy(f32[1,2,2000,128]{3,2,1,0:T(8,128)} %shard_map.96) | data formatting | bytes 4096000
Async XLA Ops:
  99.4 103.9 %copy-start = (f32[56,1536]{1,0:T(8,128)S(1)}, f32[56,1536]{1,0:T(8,128)}, u32[]{:S(2)}) copy-start(f32[56,1536]{1,0:T(8,128)} %get-tuple-element.12) | copy-start | bytes 1032196
